TPU v7x, 32 devices: a whole 2x2x4 slice. The times are simulated.
32 devices in a mesh: probe: 2 (over y), space: 16 (over z, x, core).
Axes of the slice: x: 2, y: 2, z: 4, core: 2. Of those that a mesh axis runs over, the one named last changes fastest.
Arguments:
- probe_dirs: float32 [8, 16, 256], P('probe', 'space'), may hold values from -6 to 6
- log_param: float32 [16, 256], P('space'), may hold values from -1 to 1
- background: float32 [128, 32, 512], P('space'), may hold values from 0.3 to 1.5
- site_class: int32 [128, 32, 512], P('space'), may hold values from 0 to 3
- trap_density: float32 [4], replicated, may hold values from 0.2 to 1
Outputs:
- q_basis: float32 [8, 16, 256], P('probe', 'space')
- lower_factor: float32 [8, 8], replicated
All inputs are finite; a program needn't handle non-finite values.
Results may differ from a plain program's by a relative error of at most 0.0003.
Values sent between devices are 32-bit elements; how exact they have to be, the bound alone decides.
No kernel may reach another device: no remote copies, remote signals or barrier semaphores. Data moves between devices by JAX's collectives and lax.ppermute only.
A program may use at most 64 MiB of HBM per device.

v0:
```python
import functools

import jax
import jax.numpy as jnp
from jax import lax
from jax.experimental import pallas as pl
from jax.experimental.pallas import tpu as pltpu
from jax.sharding import PartitionSpec as P

PX = 64
PY = 4
REF = 8
STEP = 0.12
HALO = 3
LANES = 128
HIGHEST = lax.Precision.HIGHEST


def dot_nn(a, b):
    return lax.dot_general(
        a, b, (((1,), (0,)), ((), ())), precision=HIGHEST, preferred_element_type=jnp.float32
    )


def dot_nt(a, b):
    return lax.dot_general(
        a, b, (((1,), (1,)), ((), ())), precision=HIGHEST, preferred_element_type=jnp.float32
    )


def parts_of(x):
    first = x.astype(jnp.bfloat16)
    rest = x - first.astype(jnp.float32)
    second = rest.astype(jnp.bfloat16)
    third = (rest - second.astype(jnp.float32)).astype(jnp.bfloat16)
    return first, second, third


def bf16_dot(a, b):
    return jnp.dot(a, b, preferred_element_type=jnp.float32)


def interleave(background, sites, order, bg, site):
    count = background.shape[0]
    parts = list(parts_of(background)) + [sites.astype(jnp.bfloat16)]
    placed = bf16_dot(jnp.concatenate(parts, axis=0), order[...])
    for k in range(bg.shape[0]):
        columns = placed[:, k * LANES : (k + 1) * LANES]
        both = columns[:count] + columns[count : 2 * count]
        bg[k] = both + columns[2 * count : 3 * count]
        site[k] = columns[3 * count :]


def cell_matrix(chunks, turned=False):
    half = REF // chunks
    dims = (LANES, PX * PY) if turned else (PX * PY, LANES)
    cell = lax.broadcasted_iota(jnp.int32, dims, int(turned)) % PX
    lane = lax.broadcasted_iota(jnp.int32, dims, 1 - int(turned)) // half
    return jnp.where(cell == lane, 1.0, 0.0).astype(jnp.float32)


def own_cells(folds):
    half = REF // folds
    sublane = lax.broadcasted_iota(jnp.int32, (8, PX * PY), 0) // half
    return lax.broadcasted_iota(jnp.int32, (8, PX * PY), 1) // PX == sublane


def prolonged(coarse, folds, chunks):
    mask = own_cells(folds)
    rows = [jnp.where(mask, coarse[n : n + 1, :], 0.0) for n in range(coarse.shape[0])]
    return cell_dot(jnp.concatenate(rows, axis=0), cell_matrix(chunks))


def cell_dot(rows, matrix):
    count = rows.shape[0]
    parts = jnp.concatenate(float_parts(rows), axis=0).astype(jnp.bfloat16)
    placed = bf16_dot(parts, matrix.astype(jnp.bfloat16))
    return (placed[:count] + placed[count : 2 * count]) + placed[2 * count :]


def float_parts(x):
    first = x.astype(jnp.bfloat16).astype(jnp.float32)
    rest = x - first
    second = rest.astype(jnp.bfloat16).astype(jnp.float32)
    return first, second, rest - second


def cell_order(columns, chunks):
    x = lax.broadcasted_iota(jnp.int32, (columns, columns), 0)
    place = lax.broadcasted_iota(jnp.int32, (columns, columns), 1)
    wanted = chunks * (place % LANES) + place // LANES
    return jnp.where(x == wanted, 1.0, 0.0).astype(jnp.bfloat16)


def spread_cells(dirs, log_param, folds, chunks):
    probes = dirs.shape[0]
    coarse = [dirs[p] for p in range(probes)] + [jnp.exp(log_param[...])]
    spread = prolonged(jnp.concatenate(coarse, axis=0), folds, chunks)
    return [spread[8 * n : 8 * n + 8, :] for n in range(probes + 1)]


def weights_and_sources(density, scale, background, sites, planes, order, bg, site, store):
    first, count = planes
    rows, columns = background.shape[1:]
    chunks, folds = columns // LANES, rows // 8
    at = pl.ds(first, count)
    cells = (count * rows, columns)
    interleave(
        background[at].reshape(cells),
        sites[at].reshape(cells).astype(jnp.float32),
        order,
        bg,
        site,
    )
    for z in range(count):
        for r in range(folds):
            for k in range(chunks):
                row = pl.ds(z * rows + r, 8, stride=folds)
                kind = site[k, row, :]
                trap = jnp.full((8, LANES), density[density.shape[0] - 1])
                for n in range(density.shape[0] - 2, -1, -1):
                    trap = jnp.where(kind == float(n), density[n], trap)
                trap = trap * scale
                weight = (1.0 / STEP - 6.0) - trap
                store(first + z, r * chunks + k, weight, -STEP * trap * bg[k, row, :])


def packet_kernel(
    density, background_in, sites_in, log_param_in, dirs_in, packet,
    background, sites, log_param, dirs, order, bg, site, made, sems, out_sems,
):
    rows, columns = background.shape[1:]
    chunks, folds = columns // LANES, rows // 8
    tiles = chunks * folds
    probes = dirs.shape[0]
    pairs = [
        (log_param_in, log_param),
        (dirs_in, dirs),
        (background_in.at[pl.ds(0, 2 * HALO)], background),
        (sites_in.at[pl.ds(0, 2 * HALO)], sites),
    ]
    copies = [pltpu.make_async_copy(a, b, sems.at[n]) for n, (a, b) in enumerate(pairs)]
    for copy in copies:
        copy.start()
    order[...] = cell_order(columns, chunks)
    copies[0].wait()
    copies[1].wait()
    spread = spread_cells(dirs, log_param, folds, chunks)
    for p in range(probes):
        made[p] = spread[p]

    first_weight = probes + 2 * HALO * tiles
    ranges = {
        HALO - 1: [(0, probes + HALO * tiles), (first_weight, HALO * tiles)],
        2 * HALO - 1: [
            (probes + HALO * tiles, HALO * tiles),
            (first_weight + HALO * tiles, (HALO - 1) * tiles),
        ],
    }
    sent = []

    def store(z, t, weight, source):
        made[probes + z * tiles + t] = source
        if z < 2 * HALO - 1:
            made[probes + (2 * HALO + z) * tiles + t] = weight
        if t == tiles - 1:
            for start, length in ranges.get(z, []):
                at = pl.ds(start, length)
                copy = pltpu.make_async_copy(made.at[at], packet.at[at], out_sems.at[len(sent)])
                copy.start()
                sent.append(copy)

    copies[2].wait()
    copies[3].wait()
    weights_and_sources(
        density, spread[probes], background, sites, (0, 2 * HALO), order, bg, site, store
    )
    for copy in sent:
        copy.wait()


class Steps:
    def __init__(self, chunks, folds, probes, zero_plane, coef, src):
        self.chunks, self.folds, self.tiles = chunks, folds, chunks * folds
        self.probes, self.zero_plane = probes, zero_plane
        self.coef, self.src = coef, src
        self.lane = lax.broadcasted_iota(jnp.int32, (8, LANES), 1)
        self.sublane = lax.broadcasted_iota(jnp.int32, (8, LANES), 0)

    def clear(self, *fields):
        nothing = jnp.zeros((8, LANES), jnp.float32)
        for t in range(self.tiles):
            for field in fields:
                for p in range(self.probes):
                    field[self.zero_plane, p, t] = nothing

    def from_left(self, x):
        return jnp.where(self.lane == 0, 0.0, pltpu.roll(x, 1, 1))

    def from_right(self, x):
        return jnp.where(self.lane == LANES - 1, 0.0, pltpu.roll(x, LANES - 1, 1))

    def from_before(self, x):
        return jnp.where(self.sublane == 0, 0.0, pltpu.roll(x, 1, 0))

    def from_after(self, x):
        return jnp.where(self.sublane == 7, 0.0, pltpu.roll(x, 7, 0))

    def first(self, own, to, other=None, beyond=()):
        chunks, folds, tiles = self.chunks, self.folds, self.tiles
        src, coef = self.src, self.coef
        turns = (self.from_left, self.from_right, self.from_before, self.from_after)
        shifted = [[f(x) for x in own] for f in turns]

        def body(z, carry):
            down = jnp.where(z > 0, z - 1, self.zero_plane) * tiles
            up = (z + 1) * tiles
            s = [[src[z * tiles + r * chunks + k] for k in range(chunks)] for r in range(folds)]
            for r in range(folds):
                for k in range(chunks):
                    t = r * chunks + k
                    same = coef[z * tiles + t] * s[r][k]
                    outer = []
                    for there, value, turn, kind in (
                        (k > 0, s[r][k - 1], (1, 1), 0),
                        (k + 1 < chunks, s[r][(k + 1) % chunks], (LANES - 1, 1), 1),
                        (r > 0, s[r - 1][k], (1, 0), 2),
                        (r + 1 < folds, s[(r + 1) % folds][k], (7, 0), 3),
                    ):
                        if there:
                            same = same + value
                        else:
                            outer.append((pltpu.roll(value, *turn), shifted[kind]))
                    for name, value in (("down", src[down + t]), ("up", src[up + t])):
                        if name == other:
                            outer.append((value, beyond))
                        else:
                            same = same + value
                    for p in range(self.probes):
                        result = same * own[p]
                        for value, factor in outer:
                            result = result + value * factor[p]
                        to[z, p, t] = result
            return carry

        return body

    def stencil(self, ref, valid, z, emit, extra):
        chunks, folds, tiles = self.chunks, self.folds, self.tiles
        first, stop = valid

        def at(z):
            return jnp.where((z >= first) & (z < stop), z, self.zero_plane)

        down, here, there, up = at(z - 1), at(z), at(z + 1), at(z + 2)
        for p in range(self.probes):
            pair = [[ref[plane, p, t] for t in range(tiles)] for plane in (here, there)]
            for r in range(folds):
                for k in range(chunks):
                    t = r * chunks + k
                    for n, value in enumerate(pair):
                        left = value[t - 1] if k else self.from_left(value[t + chunks - 1])
                        if k + 1 < chunks:
                            right = value[t + 1]
                        else:
                            right = self.from_right(value[t + 1 - chunks])
                        if r:
                            before = value[t - chunks]
                        else:
                            before = self.from_before(value[t + tiles - chunks])
                        if r + 1 < folds:
                            after = value[t + chunks]
                        else:
                            after = self.from_after(value[t + chunks - tiles])
                        above = pair[1 - n][t] + (ref[up, p, t] if n else ref[down, p, t])
                        weight = self.coef[(z + n) * tiles + t]
                        if extra:
                            weight = weight + extra
                        sides = (left + right) + (before + after)
                        emit(z + n, p, t, (sides + above) + weight * value[t])

    def step(self, ref, to, valid, wanted, extra=0.0):
        start, stop = wanted

        def body(n, carry):
            def emit(z, p, t, result):
                to[z, p, t] = result

            self.stencil(ref, valid, jnp.minimum(start + 2 * n, stop - 2), emit, extra)
            return carry

        lax.fori_loop(0, (stop - start + 1) // 2, body, 0)

    def widen(self, ref, to, valid, at_low, at_high):
        first, stop = valid

        def move(a, b):
            for p in range(self.probes):
                for t in range(self.tiles):
                    to[b, p, t] = ref[a, p, t]

        pl.when(at_low)(lambda: move(first, first - 1))
        pl.when(at_high)(lambda: move(stop - 1, stop))

    def images(self, m, u, by_one, by_two, span, carry, other=None):
        chunks, folds, tiles = self.chunks, self.folds, self.tiles
        src = self.src

        def at(z, valid):
            return jnp.where((z >= valid[0]) & (z < valid[1]), z, self.zero_plane)

        def body(z, carry):
            carry = [list(c) for c in carry]
            down = jnp.where(z > 0, z - 1, self.zero_plane) * tiles
            up = (z + 1) * tiles
            here, kept = at(z, by_one), at(z, by_two)
            s = [src[z * tiles + t] for t in range(tiles)]
            for t in range(tiles):
                r, k = t // chunks, t % chunks
                same = self.coef[z * tiles + t] * s[t]
                moved = []
                if k:
                    same = same + s[t - 1]
                else:
                    moved.append((2, self.from_left(s[t + chunks - 1])))
                if k + 1 < chunks:
                    same = same + s[t + 1]
                else:
                    moved.append((1, self.from_right(s[t + 1 - chunks])))
                if r:
                    same = same + s[t - chunks]
                else:
                    moved.append((4, self.from_before(s[t + tiles - chunks])))
                if r + 1 < folds:
                    same = same + s[t + chunks]
                else:
                    moved.append((3, self.from_after(s[t + chunks - tiles])))
                for name, value in (("down", src[down + t]), ("up", src[up + t])):
                    if name == other:
                        moved.append((5, value))
                    else:
                        same = same + value
                scaled = s[t] * (1.0 / STEP**2)
                for p in range(self.probes):
                    value = m[here, p, t]
                    carry[p][0] = carry[p][0] + (same * value + scaled * u[kept, p, t])
                    for n, factor in moved:
                        carry[p][n] = carry[p][n] + factor * value
            return tuple(tuple(c) for c in carry)

        if isinstance(span, int):
            return body(span, carry)
        return lax.fori_loop(*span, body, carry)

    def empty_sums(self):
        nothing = jnp.zeros((8, LANES), jnp.float32)
        return ((nothing,) * 6,) * self.probes

    def moved_sums(self, sums):
        return [
            c[0]
            + (self.from_left(c[1]) + self.from_right(c[2]))
            + (self.from_before(c[3]) + self.from_after(c[4]))
            for c in sums
        ]

    def after_tangent(self, odd, even, mine, at_low, at_high):
        first, stop = mine
        by_two = (jnp.where(at_low, first - 1, first), jnp.where(at_high, stop + 1, stop))
        by_one = (jnp.where(at_low, first - 2, first), jnp.where(at_high, stop + 2, stop))
        self.step(odd, even, mine, mine, 1.0 / STEP)
        self.widen(odd, even, mine, at_low, at_high)
        self.step(even, odd, by_two, by_two)
        self.widen(even, odd, by_two, at_low, at_high)
        return by_one, by_two


def inner_kernel(
    edge, density, background_in, sites_in, log_param_in, dirs_in,
    coef, src, wide, kept, sums,
    background, sites, log_param, dirs, order, bg, site, even, odd, sems,
):
    planes, rows, columns = background.shape
    chunks, folds = columns // LANES, rows // 8
    tiles = chunks * folds
    probes = dirs.shape[0]
    copies = [
        (log_param_in, log_param),
        (dirs_in, dirs),
        (background_in, background),
        (sites_in, sites),
    ]
    copies = [pltpu.make_async_copy(a, b, sems.at[n]) for n, (a, b) in enumerate(copies)]
    for copy in copies:
        copy.start()
    steps = Steps(chunks, folds, probes, planes, coef, src)
    steps.clear(even, odd)
    nothing = jnp.zeros((8, LANES), jnp.float32)
    for t in range(tiles):
        src[planes * tiles + t] = nothing
    order[...] = cell_order(columns, chunks)
    for copy in copies:
        copy.wait()
    spread = spread_cells(dirs, log_param, folds, chunks)
    for p in range(probes):
        wide[p] = spread[p]

    def store(z, t, weight, source):
        coef[z * tiles + t] = weight
        src[z * tiles + t] = source

    weights_and_sources(
        density, spread[probes], background, sites, (0, planes), order, bg, site, store
    )
    at_low = edge[0] != 0

    def low(z):
        return jnp.where(at_low, z, 0)

    last = planes - HALO
    lax.fori_loop(low(1), last + 2, steps.first(spread[:probes], odd), 0)
    steps.step(odd, even, (low(1), last + 2), (low(2), last + 1))
    for n, (ref, z) in enumerate(((odd, last), (odd, last + 1), (even, last - 1), (even, last))):
        for p in range(probes):
            for t in range(tiles):
                kept[n, p, t] = ref[z, p, t]
    mine = (low(HALO), last)
    steps.step(even, odd, (low(2), last + 1), mine)
    by_one, by_two = steps.after_tangent(odd, even, mine, at_low, True)
    result = steps.moved_sums(steps.images(odd, even, by_one, by_two, by_one, steps.empty_sums()))
    for p in range(probes):
        sums[p] = result[p]


def outer_kernel(
    chunks, folds, edge, own_coef, own_src, own_wide, kept, own_sums, packet, out,
    coef, src, even, odd,
):
    tiles = chunks * folds
    probes = own_wide.shape[0]
    total = even.shape[0] - 1
    planes = total - 2 * HALO
    steps = Steps(chunks, folds, probes, total, coef, src)
    last = planes - HALO
    halo = planes * tiles

    def copy(source, start, target, at, count):
        def body(n, carry):
            for t in range(tiles):
                target[at + n * tiles + t] = source[start + n * tiles + t]
            return carry

        lax.fori_loop(0, count, body, 0)

    own = (last - HALO) * tiles
    copy(own_src, own, src, own, planes - last + HALO)
    copy(own_coef, own, coef, own, planes - last + HALO)
    copy(packet, probes, src, halo, 2 * HALO)
    copy(packet, probes + 2 * HALO * tiles, coef, halo, 2 * HALO - 1)
    steps.clear(even, odd)
    for p in range(probes):
        for t in range(tiles):
            odd[last, p, t] = kept[0, p, t]
            odd[last + 1, p, t] = kept[1, p, t]
            even[last - 1, p, t] = kept[2, p, t]
            even[last, p, t] = kept[3, p, t]

    at_high = edge[1] != 0

    def high(z):
        return jnp.where(at_high, z, planes)

    mine = [own_wide[p] for p in range(probes)]
    beyond = [packet[p] for p in range(probes)]
    steps.first(mine, odd, "up", beyond)(planes - 1, 0)

    @pl.when(at_high)
    def _():
        steps.first(beyond, odd, "down", mine)(planes, 0)
        lax.fori_loop(planes + 1, total - 1, steps.first(beyond, odd), 0)

    steps.step(odd, even, (last, high(total - 1)), (last + 1, high(total - 2)))
    mine = (last, high(total - HALO))
    steps.step(even, odd, (last - 1, high(total - 2)), mine)
    by_one, by_two = steps.after_tangent(odd, even, mine, True, at_high)
    start, stop = by_one
    empty = steps.empty_sums()
    inside = steps.images(odd, even, by_one, by_two, (start, planes - 1), empty)
    inside = steps.images(odd, even, by_one, by_two, planes - 1, inside, "up")
    above = [list(c) for c in empty]
    for p in range(probes):
        above[p][0] = inside[p][5]
    above = steps.images(odd, even, by_one, by_two, (planes + 1, stop), tuple(tuple(c) for c in above))
    above = steps.images(odd, even, by_one, by_two, planes, above, "down")
    inside = [x + own_sums[p] + above[p][5] for p, x in enumerate(steps.moved_sums(inside))]
    above = steps.moved_sums(above)

    added = jnp.concatenate(inside + above, axis=0) * STEP**6
    images = cell_dot(added, cell_matrix(chunks, True))
    mask = own_cells(folds)
    for part in range(2):
        halves = []
        for p in range(probes):
            image = jnp.where(mask, images[8 * (part * probes + p) :][:8], 0.0)
            image = jnp.sum(image, axis=0, keepdims=True)
            halves += [image[:, h * LANES : (h + 1) * LANES] for h in range(image.shape[1] // LANES)]
        halves = jnp.concatenate(halves, axis=0)

        def send(n, carry):
            out[n, part] = halves
            return carry

        lax.fori_loop(0, out.shape[0], send, 0, unroll=8)


def eliminate(gram):
    count = gram.shape[0]
    rows = lax.broadcasted_iota(jnp.int32, (count, count), 0)
    columns = lax.broadcasted_iota(jnp.int32, (count, count), 1)
    inverse = jnp.where(rows == columns, 1.0, 0.0)
    for j in range(count - 1):
        across = jnp.broadcast_to(gram[:, j : j + 1], (count, count))
        turned = 1.0 / across
        ratio = jnp.where(rows > j, across, 0.0)
        gram_row, inverse_row = (gram * turned)[j : j + 1, :], (inverse * turned)[j : j + 1, :]
        gram = gram - ratio * gram_row
        inverse = inverse - ratio * inverse_row
    diagonal = jnp.sum(jnp.where(rows == columns, gram, 0.0), axis=1, keepdims=True)
    scale = 1.0 / jnp.sqrt(diagonal)
    upper = jnp.where(columns >= rows, gram, 0.0) * scale
    return upper, inverse * scale


def gram_of(parts, count):
    stacked = jnp.concatenate(list(parts) + [jnp.zeros_like(parts[0])], axis=0)
    stacked = stacked.astype(jnp.bfloat16)
    every = lax.dot_general(
        stacked, stacked, (((1,), (1,)), ((), ())), preferred_element_type=jnp.float32
    )
    tall = every[:count] + (every[count : 2 * count] + every[2 * count : 3 * count])
    return tall[:, :count] + (tall[:, count : 2 * count] + tall[:, 2 * count : 3 * count])


def times(a, parts):
    first, second, third = float_parts(a)
    left = jnp.concatenate([first, second, third, first, second, first], axis=1)
    right = jnp.concatenate([parts[0]] * 3 + [parts[1]] * 2 + [parts[2]], axis=0)
    return bf16_dot(left.astype(jnp.bfloat16), right.astype(jnp.bfloat16))


def factor_kernel(place, parts, q_out, lower_out, rows_ref, q_ref):
    groups, slabs, _, probes, cells = parts.shape
    count = groups * probes
    for g in range(groups):

        def gather(slab, carry):
            before = jnp.maximum(slab - 1, 0)
            image = parts[g, slab, 0] + jnp.where(slab > 0, parts[g, before, 1], 0.0)
            at = pl.multiple_of(slab * cells, cells)
            rows_ref[pl.ds(g * probes, probes), pl.ds(at, cells)] = image
            return carry

        lax.fori_loop(0, slabs, gather, 0, unroll=True if slabs <= 16 else 8)
    total = slabs * cells
    rows = rows_ref[...]
    parts_one = float_parts(rows)
    upper_one, inverse_one = eliminate(gram_of(parts_one, count) / total)
    basis = times(inverse_one, parts_one)
    rows_ref[...] = basis
    upper_two, inverse_two = eliminate(gram_of(float_parts(basis), count) / total)
    mine = rows_ref[:, pl.ds(pl.multiple_of(place[1] * cells, cells), cells)]
    q_ref[...] = dot_nn(inverse_two, mine)
    for g in range(groups):

        @pl.when(place[0] == g)
        def _():
            q_out[:, 0, :] = q_ref[pl.ds(g * probes, probes), :]

    r = lax.broadcasted_iota(jnp.int32, (count, count), 0)
    c = lax.broadcasted_iota(jnp.int32, (count, count), 1)
    lower_one = dot_nt(jnp.where(r == c, 1.0, 0.0), upper_one)
    lower_out[...] = dot_nt(lower_one, upper_two)


def everywhere(x):
    x = jnp.broadcast_to(jnp.sum(x, axis=1, keepdims=True), x.shape)
    for shift in (4, 2, 1):
        x = x + pltpu.roll(x, shift, 0)
    return x


def cholesky(rows, total):
    count = len(rows)
    rows = [list(row) for row in rows]
    gram = {}
    for i in range(count):
        for j in range(i + 1):
            product = sum(a * b for a, b in zip(rows[i][1:], rows[j][1:]))
            gram[i, j] = everywhere(rows[i][0] * rows[j][0] + product) * (1.0 / total)
    factor = {}
    for j in range(count):
        pivot = gram[j, j]
        turned = lax.rsqrt(pivot)
        turned = turned * (1.5 - 0.5 * pivot * turned * turned)
        factor[j, j] = pivot * turned
        rows[j] = [x * turned for x in rows[j]]
        for i in range(j + 1, count):
            factor[i, j] = gram[i, j] * turned
        for i in range(j + 1, count):
            for k in range(j + 1, i + 1):
                gram[i, k] = gram[i, k] - factor[i, j] * factor[k, j]
            rows[i] = [x - factor[i, j] * y for x, y in zip(rows[i], rows[j])]
    return factor, rows


def register_kernel(groups, slabs, probes, place, parts, q_out, lower_out, q_ref):
    halves = q_out.shape[2] // LANES
    pieces = probes * halves
    step = 2 * pieces
    sublane = lax.broadcasted_iota(jnp.int32, (8, LANES), 0)
    rows = []
    for g in range(groups):
        for p in range(probes):
            row = []
            for block in range(slabs // 8):
                for h in range(halves):
                    at = (8 * block * groups + g) * step + p * halves + h
                    own = parts[pl.ds(at, 8, stride=groups * step), :]
                    if block:
                        before = parts[pl.ds(at + pieces - groups * step, 8, stride=groups * step), :]
                    else:
                        before = parts[pl.ds(at + pieces, 8, stride=groups * step), :]
                        before = jnp.where(sublane == 0, 0.0, pltpu.roll(before, 1, 0))
                    row.append(own + before)
            rows.append(row)
    total = slabs * halves * LANES
    factor_one, basis = cholesky(rows, total)
    factor_two, rows = cholesky(basis, total)
    for i, row in enumerate(rows):
        for n, x in enumerate(row):
            q_ref[i, n % halves, pl.ds(8 * (n // halves), 8), :] = x
    for p in range(probes):
        for h in range(halves):
            mine = q_ref[place[0] * probes + p, h, pl.ds(place[1], 1), :]
            q_out[p, :, pl.ds(h * LANES, LANES)] = mine
    count = len(rows)
    r = lax.broadcasted_iota(jnp.int32, (8, LANES), 0)
    c = lax.broadcasted_iota(jnp.int32, (8, LANES), 1)
    lower = jnp.zeros((8, LANES), jnp.float32)
    for i in range(count):
        for j in range(i + 1):
            entry = sum(factor_one[i, k] * factor_two[k, j] for k in range(j, i + 1))
            lower = jnp.where((r == i) & (c == j), entry, lower)
    lower_out[...] = lower[:count, :count]


def shards(probe_dirs, log_param, background, site_class, trap_density):
    probes = probe_dirs.shape[0]
    cells = probe_dirs.shape[2]
    planes, rows, columns = background.shape
    slabs = lax.axis_size("space")
    groups = lax.axis_size("probe")
    at_space = lax.axis_index("space")
    vmem = pl.BlockSpec(memory_space=pltpu.VMEM)
    smem = pl.BlockSpec(memory_space=pltpu.SMEM)
    anywhere = pl.BlockSpec(memory_space=pl.ANY)
    params = pltpu.CompilerParams(vmem_limit_bytes=62 * 2**20)

    chunks, folds = columns // LANES, rows // 8
    tiles = chunks * folds
    total = planes + 2 * HALO
    tile = (8, LANES)

    def shape(*dims):
        return jax.ShapeDtypeStruct(dims + tile, jnp.float32)

    def scratch(*dims):
        return pltpu.VMEM(dims + tile, jnp.float32)

    def copies(count):
        return pltpu.SemaphoreType.DMA((count,))

    def inputs(held):
        return [
            pltpu.VMEM((held, rows, columns), jnp.float32),
            pltpu.VMEM((held, rows, columns), jnp.int32),
            pltpu.VMEM(log_param.shape, jnp.float32),
            pltpu.VMEM(probe_dirs.shape, jnp.float32),
            pltpu.VMEM((columns, columns), jnp.bfloat16),
        ]

    def rows_of(held):
        return pltpu.VMEM((chunks, held * rows, LANES), jnp.float32)

    size = probes + (4 * HALO - 1) * tiles
    packet = pl.pallas_call(
        packet_kernel,
        out_shape=shape(size),
        in_specs=[smem] + [anywhere] * 4,
        out_specs=anywhere,
        scratch_shapes=inputs(2 * HALO)
        + [rows_of(2 * HALO), rows_of(2 * HALO), scratch(size), copies(4), copies(4)],
        compiler_params=params,
        name="packet",
    )(trap_density, background, site_class, log_param, probe_dirs)

    down = [(i + 1, i) for i in range(slabs - 1)]
    next_packet = lax.ppermute(packet, "space", down)
    edge = jnp.stack([at_space > 0, at_space < slabs - 1]).astype(jnp.int32)
    own_coef, own_src, wide, kept, sums = pl.pallas_call(
        inner_kernel,
        out_shape=(
            shape(planes * tiles),
            shape((planes + 1) * tiles),
            shape(probes),
            shape(4, probes, tiles),
            shape(probes),
        ),
        in_specs=[smem, smem] + [anywhere] * 4,
        out_specs=(vmem,) * 5,
        scratch_shapes=inputs(planes)
        + [rows_of(planes), rows_of(planes)]
        + [scratch(planes + 1, probes, tiles)] * 2
        + [copies(4)],
        compiler_params=pltpu.CompilerParams(vmem_limit_bytes=28 * 2**20),
        cost_estimate=pl.CostEstimate(flops=10**9, bytes_accessed=2**24, transcendentals=256),
        name="inner",
    )(edge, trap_density, background, site_class, log_param, probe_dirs)

    pieces = probes * cells // LANES
    images = pl.pallas_call(
        functools.partial(outer_kernel, chunks, folds),
        out_shape=jax.ShapeDtypeStruct((groups * slabs, 2, pieces, LANES), jnp.float32),
        in_specs=[smem] + [vmem] * 6,
        out_specs=vmem,
        scratch_shapes=[
            scratch(total * tiles),
            scratch(total * tiles),
            scratch(total + 1, probes, tiles),
            scratch(total + 1, probes, tiles),
        ],
        compiler_params=pltpu.CompilerParams(vmem_limit_bytes=28 * 2**20),
        name="outer",
    )(edge, own_coef, own_src, wide, kept, sums, next_packet)

    every = lax.all_to_all(images, ("space", "probe"), split_axis=0, concat_axis=0, tiled=True)
    place = jnp.stack([lax.axis_index("probe"), at_space]).astype(jnp.int32)
    count = groups * probes
    results = (
        jax.ShapeDtypeStruct((probes, 1, cells), jnp.float32),
        jax.ShapeDtypeStruct((count, count), jnp.float32),
    )
    params = pltpu.CompilerParams(vmem_limit_bytes=28 * 2**20)
    if count <= 8 and slabs % 8 == 0:
        halves = cells // LANES
        return pl.pallas_call(
            functools.partial(register_kernel, groups, slabs, probes),
            out_shape=results,
            in_specs=[smem, vmem],
            out_specs=(vmem, vmem),
            scratch_shapes=[pltpu.VMEM((count, halves, slabs, LANES), jnp.float32)],
            compiler_params=params,
            name="factor",
        )(place, every.reshape((groups * slabs * 2 * pieces, LANES)))
    return pl.pallas_call(
        factor_kernel,
        out_shape=results,
        in_specs=[smem, vmem],
        out_specs=(vmem, vmem),
        scratch_shapes=[
            pltpu.VMEM((count, slabs * cells), jnp.float32),
            pltpu.VMEM((count, cells), jnp.float32),
        ],
        compiler_params=params,
        name="factor",
    )(place, every.reshape((slabs, groups, 2, probes, cells)).swapaxes(0, 1))


def solution(mesh):
    placed = (
        P("probe", "space", None),
        P("space", None),
        P("space", None, None),
        P("space", None, None),
        P(),
    )
    return jax.shard_map(
        shards,
        mesh=mesh,
        in_specs=placed,
        out_specs=(P("probe", "space", None), P()),
        check_vma=False,
    )
```

profile of v0, /device:TPU:0, one launch (start us, length us, event | category | flops | bytes accessed | tf_op | source)
XLA Modules:
  0.0 41.5 jit_solution(658224058466335888)
XLA Ops:
  0.6 0.0 copy-start.1
  0.6 0.0 copy-start
  0.6 3.5 %packet.1 = f32[180,8,128]{2,1,0:T(8,128)} custom-call(f32[4]{0:T(128)} %density.3, f32[8,32,512]{2,1,0:T(8,128)} %background_in.3, s32[8,32,512]{2,1,0:T(8,128)} %sites_in.3, f32[1,256]{1,0:T(1,128)} %log_param_in.3, f32[4,1,256]{2,1,0:T(1,128)} %dirs_in.3), custom_call_target="tpu_custom_call" | custom-call | tf_op jit(solution)/shard_map/packet/pallas_call | solution.py:696
  4.1 1.3 %collective-permute-start = (f32[180,8,128]{2,1,0:T(8,128)}, f32[180,8,128]{2,1,0:T(8,128)S(1)}, u32[]{:S(2)}, u32[]{:S(2)}) collective-permute-start(f32[180,8,128]{2,1,0:T(8,128)} %packet.1), channel_id=1, source_target_pairs={{1,0},{2,1},{3,2},{4,3},{5,4},{6,5},{7,6},{8,7},{9,8},{10,9},{11,1... | collective-permute-start | bytes 2211848 | tf_op jit(solution)/shard_map/ppermute | solution.py:708
  5.4 0.0 copy-start.2
  5.4 0.0 copy-start.3
  5.5 0.0 copy-start.4
  5.5 0.1 add_convert_fusion.edge
  5.5 0.0 copy-done.1
  5.5 0.0 copy-done
  5.5 0.6 %copy-done.2 = f32[4,1,256]{2,1,0:T(1,128)S(1)} copy-done((f32[4,1,256]{2,1,0:T(1,128)S(1)}, f32[4,1,256]{2,1,0:T(1,128)}, u32[]{:S(2)}) %copy-start.2) | copy-done | bytes 4120
  6.1 0.0 copy-done.3
  6.1 0.0 copy-done.4
  6.1 5.7 %inner.1 = (f32[128,8,128]{2,1,0:T(8,128)S(1)}, f32[144,8,128]{2,1,0:T(8,128)S(1)}, f32[4,8,128]{2,1,0:T(8,128)S(1)}, f32[4,4,16,8,128]{4,3,2,1,0:T(8,128)S(1)}, f32[4,8,128]{2,1,0:T(8,128)S(1)}) custom-call(s32[2]{0:T(128)S(1)} %add_convert_fusion.edge, f32[4]{0:T(128)S(1)} %copy-done.4, f32[8,32,512]{2,1,0:T(8,128)S(1)} %copy-done, ...), custom_call_target="tpu_custom_call" | custom-call | flops 1000000000 | bytes 16777216 | tf_op jit(solution)/shard_map/inner/pallas_call | solution.py:710
  11.9 0.0 collective-permute-done.packet
  11.9 5.5 %outer.1 = f32[32,2,8,128]{3,2,1,0:T(8,128)} custom-call(s32[2]{0:T(128)S(1)} %add_convert_fusion.edge, f32[128,8,128]{2,1,0:T(8,128)S(1)} %get-tuple-element.7.own_coef, f32[144,8,128]{2,1,0:T(8,128)S(1)} %get-tuple-element.8.own_src, f32[4,8,128]{2,1,0:T(8,128)S(1)} %get-tuple-element.9.own_wide, f32[4,4,16,8,128]{4,3,2,1,0:T(8,128)S(1)} %get-tuple-element.10.kept, ...), custom_call_target="tpu_custom_call" | custom-call | tf_op jit(solution)/shard_map/outer/pallas_call | solution.py:731
  17.3 11.8 %all-to-all-start = ((f32[32,2,8,128]{3,2,1,0:T(8,128)}), f32[32,2,8,128]{3,2,1,0:T(8,128)S(1)}, u32[]{:S(2)}, u32[]{:S(2)}) async-start(f32[32,2,8,128]{3,2,1,0:T(8,128)} %outer.1), calls=%async_computation | async-start | bytes 524288 | tf_op jit(solution)/shard_map/all_to_all | solution.py:746
  29.2 0.1 pad_add_fusion.place
  29.3 10.6 %all-to-all-done = f32[32,2,8,128]{3,2,1,0:T(8,128)S(1)} async-done(((f32[32,2,8,128]{3,2,1,0:T(8,128)}), f32[32,2,8,128]{3,2,1,0:T(8,128)S(1)}, u32[]{:S(2)}, u32[]{:S(2)}) %all-to-all-start) | async-done | bytes 262176 | tf_op jit(solution)/shard_map/all_to_all | solution.py:746
  39.9 1.6 %factor.1 = (f32[4,1,256]{2,1,0:T(1,128)}, f32[8,8]{1,0:T(8,128)}) custom-call(s32[2]{0:T(128)S(1)} %pad_add_fusion.place, f32[512,128]{1,0:T(8,128)S(1)} %bitcast.5), custom_call_target="tpu_custom_call" | custom-call | tf_op jit(solution)/shard_map/factor/pallas_call | solution.py:756
Async XLA Ops:
  0.6 4.9 %copy-start.1 = (s32[8,32,512]{2,1,0:T(8,128)S(1)}, s32[8,32,512]{2,1,0:T(8,128)}, u32[]{:S(2)}) copy-start(s32[8,32,512]{2,1,0:T(8,128)} %sites_in.3) | copy-start | bytes 1572868
  0.6 4.9 %copy-start = (f32[8,32,512]{2,1,0:T(8,128)S(1)}, f32[8,32,512]{2,1,0:T(8,128)}, u32[]{:S(2)}) copy-start(f32[8,32,512]{2,1,0:T(8,128)} %background_in.3) | copy-start | bytes 1572868
  4.1 7.8 %collective-permute-start = (f32[180,8,128]{2,1,0:T(8,128)}, f32[180,8,128]{2,1,0:T(8,128)S(1)}, u32[]{:S(2)}, u32[]{:S(2)}) collective-permute-start(f32[180,8,128]{2,1,0:T(8,128)} %packet.1), channel_id=1, source_target_pairs={{1,0},{2,1},{3,2},{4,3},{5,4},{6,5},{7,6},{8,7},{9,8},{10,9},{11,1... | collective-permute-start | bytes 2211848 | tf_op jit(solution)/shard_map/ppermute | solution.py:708
  5.4 0.7 %copy-start.2 = (f32[4,1,256]{2,1,0:T(1,128)S(1)}, f32[4,1,256]{2,1,0:T(1,128)}, u32[]{:S(2)}) copy-start(f32[4,1,256]{2,1,0:T(1,128)} %dirs_in.3) | copy-start | bytes 12292
  5.4 0.7 %copy-start.3 = (f32[1,256]{1,0:T(1,128)S(1)}, f32[1,256]{1,0:T(1,128)}, u32[]{:S(2)}) copy-start(f32[1,256]{1,0:T(1,128)} %log_param_in.3) | copy-start | bytes 3076
  5.5 0.7 %copy-start.4 = (f32[4]{0:T(128)S(1)}, f32[4]{0:T(128)}, u32[]{:S(2)}) copy-start(f32[4]{0:T(128)} %density.3) | copy-start | bytes 52
  17.3 22.5 %all-to-all-start = ((f32[32,2,8,128]{3,2,1,0:T(8,128)}), f32[32,2,8,128]{3,2,1,0:T(8,128)S(1)}, u32[]{:S(2)}, u32[]{:S(2)}) async-start(f32[32,2,8,128]{3,2,1,0:T(8,128)} %outer.1), calls=%async_computation | async-start | bytes 524288 | tf_op jit(solution)/shard_map/all_to_all | solution.py:746
where the time goes:
time: 41.8 us; the launch traced here: 41.5 us
  Pallas kernels  16.3 us (39%)
  starting transfers between devices  13.1 us (31%)
  waiting for transfers between devices  10.6 us (25%)
  between operations  0.73 us (2%)
  local copies, waits for them, and re-layouts  0.6 us (1%)
    all_to_all x1, starting transfers between devices, shards(): lax.all_to_all(images, ('space', 'probe'), split_axis=0, concat_axis=0, t...  11.8 us
    all_to_all x1, waiting for transfers between devices, shards(): lax.all_to_all(images, ('space', 'probe'), split_axis=0, concat_axis=0, t...  10.6 us
    pallas_call x1, Pallas kernels, shards(): pl.pallas_call(inner_kernel, out_shape=(shape(planes * tiles), shape((pla...  5.74 us
    pallas_call x1, Pallas kernels, shards(): pl.pallas_call(functools.partial(outer_kernel, chunks, folds), out_shape=...  5.45 us
    pallas_call x1, Pallas kernels, shards(): pl.pallas_call(packet_kernel, out_shape=shape(size), in_specs=[smem] + [a...  3.46 us
    pallas_call x1, Pallas kernels, shards(): pl.pallas_call(functools.partial(register_kernel, groups, slabs, probes),...  1.6 us
    ppermute x1, starting transfers between devices, shards(): next_packet = lax.ppermute(packet, 'space', down)  1.29 us
  transfers between devices with their start and end apart: 2, of which 1 were waited for; matrix products, arithmetic and copies ran while one was open for 0% of the time, Pallas kernels for 14%

commit v1 on v0

--- a/solution.py
+++ b/solution.py
@@ -613,35 +613,46 @@
     return factor, rows
 
 
-def register_kernel(groups, slabs, probes, place, parts, q_out, lower_out, q_ref):
+def register_kernel(groups, slabs, probes, place, mine, other, q_out, lower_out, q_ref):
     halves = q_out.shape[2] // LANES
     pieces = probes * halves
     step = 2 * pieces
     sublane = lax.broadcasted_iota(jnp.int32, (8, LANES), 0)
+    odd = jnp.broadcast_to(place[1] % 2, (8, LANES)) == 1
+
+    def load(at):
+        at = pl.ds(at, 8, stride=step)
+        one, two = mine[at, :], other[at, :]
+        return jnp.where(odd, two, one), jnp.where(odd, one, two)
+
     rows = []
     for g in range(groups):
         for p in range(probes):
             row = []
-            for block in range(slabs // 8):
-                for h in range(halves):
-                    at = (8 * block * groups + g) * step + p * halves + h
-                    own = parts[pl.ds(at, 8, stride=groups * step), :]
-                    if block:
-                        before = parts[pl.ds(at + pieces - groups * step, 8, stride=groups * step), :]
-                    else:
-                        before = parts[pl.ds(at + pieces, 8, stride=groups * step), :]
-                        before = jnp.where(sublane == 0, 0.0, pltpu.roll(before, 1, 0))
-                    row.append(own + before)
+            for h in range(halves):
+                last = None
+                for block in range(slabs // 16):
+                    at = (g * slabs // 2 + 8 * block) * step + p * halves + h
+                    even_own, odd_own = load(at)
+                    even_next, odd_next = load(at + pieces)
+                    before = pltpu.roll(odd_next, 1, 0)
+                    first = 0.0 if last is None else last
+                    last = before
+                    row.append((block, 0, h, even_own + jnp.where(sublane == 0, first, before)))
+                    row.append((block, 1, h, odd_own + even_next))
             rows.append(row)
+    places = [x[:3] for x in rows[0]]
+    rows = [[x[3] for x in row] for row in rows]
     total = slabs * halves * LANES
     factor_one, basis = cholesky(rows, total)
     factor_two, rows = cholesky(basis, total)
     for i, row in enumerate(rows):
-        for n, x in enumerate(row):
-            q_ref[i, n % halves, pl.ds(8 * (n // halves), 8), :] = x
+        for (block, parity, h), x in zip(places, row):
+            q_ref[i, h, pl.ds(parity * (slabs // 2) + 8 * block, 8), :] = x
+    own = (place[1] % 2) * (slabs // 2) + place[1] // 2
     for p in range(probes):
         for h in range(halves):
-            mine = q_ref[place[0] * probes + p, h, pl.ds(place[1], 1), :]
+            mine = q_ref[place[0] * probes + p, h, pl.ds(own, 1), :]
             q_out[p, :, pl.ds(h * LANES, LANES)] = mine
     count = len(rows)
     r = lax.broadcasted_iota(jnp.int32, (8, LANES), 0)
@@ -730,7 +741,7 @@
     pieces = probes * cells // LANES
     images = pl.pallas_call(
         functools.partial(outer_kernel, chunks, folds),
-        out_shape=jax.ShapeDtypeStruct((groups * slabs, 2, pieces, LANES), jnp.float32),
+        out_shape=jax.ShapeDtypeStruct((groups * slabs // 2, 2, pieces, LANES), jnp.float32),
         in_specs=[smem] + [vmem] * 6,
         out_specs=vmem,
         scratch_shapes=[
@@ -743,7 +754,13 @@
         name="outer",
     )(edge, own_coef, own_src, wide, kept, sums, next_packet)
 
-    every = lax.all_to_all(images, ("space", "probe"), split_axis=0, concat_axis=0, tiled=True)
+    same = [
+        [g * slabs + z for g in range(groups) for z in range(parity, slabs, 2)] for parity in (0, 1)
+    ]
+    mine = lax.all_to_all(
+        images, ("probe", "space"), split_axis=0, concat_axis=0, axis_index_groups=same, tiled=True
+    )
+    other = lax.ppermute(mine, "space", [(z, z ^ 1) for z in range(slabs)])
     place = jnp.stack([lax.axis_index("probe"), at_space]).astype(jnp.int32)
     count = groups * probes
     results = (
@@ -751,17 +768,25 @@
         jax.ShapeDtypeStruct((count, count), jnp.float32),
     )
     params = pltpu.CompilerParams(vmem_limit_bytes=28 * 2**20)
-    if count <= 8 and slabs % 8 == 0:
+    if count <= 8 and slabs % 16 == 0:
         halves = cells // LANES
         return pl.pallas_call(
             functools.partial(register_kernel, groups, slabs, probes),
             out_shape=results,
-            in_specs=[smem, vmem],
+            in_specs=[smem, vmem, vmem],
             out_specs=(vmem, vmem),
             scratch_shapes=[pltpu.VMEM((count, halves, slabs, LANES), jnp.float32)],
             compiler_params=params,
             name="factor",
-        )(place, every.reshape((groups * slabs * 2 * pieces, LANES)))
+        )(
+            place,
+            mine.reshape((groups * slabs * pieces, LANES)),
+            other.reshape((groups * slabs * pieces, LANES)),
+        )
+    odd = at_space % 2 == 1
+    pairs = [jnp.where(odd, other, mine), jnp.where(odd, mine, other)]
+    pairs = [x.reshape((groups, slabs // 2, 2, probes, cells)) for x in pairs]
+    every = jnp.stack(pairs, axis=2).reshape((groups, slabs, 2, probes, cells))
     return pl.pallas_call(
         factor_kernel,
         out_shape=results,
@@ -773,7 +798,7 @@
         ],
         compiler_params=params,
         name="factor",
-    )(place, every.reshape((slabs, groups, 2, probes, cells)).swapaxes(0, 1))
+    )(place, every)
 
 
 def solution(mesh):

time: 41.8 us -> 39.5 us (0.945)
  blocking collectives: 0 us -> 19.8 us
  starting transfers between devices: 13.1 us -> 1.49 us
  waiting for transfers between devices: 10.6 us -> 1.08 us
  Pallas kernels: 16.3 us -> 15.5 us
    all_to_all x0 -> x1, blocking collectives: none -> 19.8 us  [shards(): lax.all_to_all(images, ('probe', 'space'), split_axis=0, concat_axis=0, a...]
    all_to_all x1 -> x0, starting transfers between devices: 11.8 us -> none  [shards(): lax.all_to_all(images, ('space', 'probe'), split_axis=0, concat_axis=0, t...]
    all_to_all x1 -> x0, waiting for transfers between devices: 10.6 us -> none  [shards(): lax.all_to_all(images, ('space', 'probe'), split_axis=0, concat_axis=0, t...]
    ppermute x0 -> x1, waiting for transfers between devices: none -> 1.08 us  [shards(): other = lax.ppermute(mine, 'space', [(z, z ^ 1) for z in range(slabs)])]
    pallas_call x1, Pallas kernels: 5.45 us -> 4.73 us  [shards(): pl.pallas_call(functools.partial(outer_kernel, chunks, folds), out_shape=...]
  transfers between devices with their start and end apart: 2 -> 2, of which waited for: 1 -> 1; matrix products, arithmetic and copies ran while one was open for 0% -> 0% of each run, Pallas kernels for 14% -> 15%
where the time goes in v1:
time: 39.5 us; the launch traced here: 39.3 us
  blocking collectives  19.8 us (50%)
  Pallas kernels  15.5 us (39%)
  starting transfers between devices  1.49 us (4%)
  waiting for transfers between devices  1.08 us (3%)
  between operations  0.73 us (2%)
  local copies, waits for them, and re-layouts  0.6 us (2%)
    all_to_all x1, blocking collectives, shards(): lax.all_to_all(images, ('probe', 'space'), split_axis=0, concat_axis=0, a...  19.8 us
    pallas_call x1, Pallas kernels, shards(): pl.pallas_call(inner_kernel, out_shape=(shape(planes * tiles), shape((pla...  5.74 us
    pallas_call x1, Pallas kernels, shards(): pl.pallas_call(functools.partial(outer_kernel, chunks, folds), out_shape=...  4.73 us
    pallas_call x1, Pallas kernels, shards(): pl.pallas_call(packet_kernel, out_shape=shape(size), in_specs=[smem] + [a...  3.46 us
    pallas_call x1, Pallas kernels, shards(): pl.pallas_call(functools.partial(register_kernel, groups, slabs, probes),...  1.57 us
    ppermute x1, starting transfers between devices, shards(): next_packet = lax.ppermute(packet, 'space', down)  1.29 us
    ppermute x1, waiting for transfers between devices, shards(): other = lax.ppermute(mine, 'space', [(z, z ^ 1) for z in range(slabs)])  1.08 us
  transfers between devices with their start and end apart: 2, of which 1 were waited for; matrix products, arithmetic and copies ran while one was open for 0% of the time, Pallas kernels for 15%

profile of v1, /device:TPU:0, one launch (start us, length us, event | category | flops | bytes accessed | tf_op | source)
XLA Modules:
  0.0 39.3 jit_solution(17130405966045310165)
XLA Ops:
  0.6 0.0 copy-start.1
  0.6 0.0 copy-start
  0.6 3.5 %packet.1 = f32[180,8,128]{2,1,0:T(8,128)} custom-call(f32[4]{0:T(128)} %density.3, f32[8,32,512]{2,1,0:T(8,128)} %background_in.3, s32[8,32,512]{2,1,0:T(8,128)} %sites_in.3, f32[1,256]{1,0:T(1,128)} %log_param_in.3, f32[4,1,256]{2,1,0:T(1,128)} %dirs_in.3), custom_call_target="tpu_custom_call" | custom-call | tf_op jit(solution)/shard_map/packet/pallas_call | solution.py:707
  4.1 1.3 %collective-permute-start = (f32[180,8,128]{2,1,0:T(8,128)}, f32[180,8,128]{2,1,0:T(8,128)S(1)}, u32[]{:S(2)}, u32[]{:S(2)}) collective-permute-start(f32[180,8,128]{2,1,0:T(8,128)} %packet.1), channel_id=1, source_target_pairs={{1,0},{2,1},{3,2},{4,3},{5,4},{6,5},{7,6},{8,7},{9,8},{10,9},{11,1... | collective-permute-start | bytes 2211848 | tf_op jit(solution)/shard_map/ppermute | solution.py:719
  5.4 0.0 copy-start.2
  5.4 0.0 copy-start.3
  5.5 0.0 copy-start.4
  5.5 0.1 add_convert_fusion.edge
  5.5 0.0 copy-done.1
  5.5 0.0 copy-done
  5.5 0.6 %copy-done.2 = f32[4,1,256]{2,1,0:T(1,128)S(1)} copy-done((f32[4,1,256]{2,1,0:T(1,128)S(1)}, f32[4,1,256]{2,1,0:T(1,128)}, u32[]{:S(2)}) %copy-start.2) | copy-done | bytes 4120
  6.1 0.0 copy-done.3
  6.1 0.0 copy-done.4
  6.1 5.7 %inner.1 = (f32[128,8,128]{2,1,0:T(8,128)S(1)}, f32[144,8,128]{2,1,0:T(8,128)S(1)}, f32[4,8,128]{2,1,0:T(8,128)S(1)}, f32[4,4,16,8,128]{4,3,2,1,0:T(8,128)S(1)}, f32[4,8,128]{2,1,0:T(8,128)S(1)}) custom-call(s32[2]{0:T(128)S(1)} %add_convert_fusion.edge, f32[4]{0:T(128)S(1)} %copy-done.4, f32[8,32,512]{2,1,0:T(8,128)S(1)} %copy-done, ...), custom_call_target="tpu_custom_call" | custom-call | flops 1000000000 | bytes 16777216 | tf_op jit(solution)/shard_map/inner/pallas_call | solution.py:721
  11.9 0.0 collective-permute-done.packet
  11.9 4.7 %outer.1 = f32[16,2,8,128]{3,2,1,0:T(8,128)S(1)} custom-call(s32[2]{0:T(128)S(1)} %add_convert_fusion.edge, f32[128,8,128]{2,1,0:T(8,128)S(1)} %get-tuple-element.7.own_coef, f32[144,8,128]{2,1,0:T(8,128)S(1)} %get-tuple-element.8.own_src, f32[4,8,128]{2,1,0:T(8,128)S(1)} %get-tuple-element.9.own_wide, f32[4,4,16,8,128]{4,3,2,1,0:T(8,128)S(1)} %get-tuple-element.10.kept, ...), custom_call_target="tpu_custom_call" | custom-call | tf_op jit(solution)/shard_map/outer/pallas_call | solution.py:742
  16.6 19.8 %all_to_all.5 = f32[16,2,8,128]{3,2,1,0:T(8,128)S(1)} all-to-all(f32[16,2,8,128]{3,2,1,0:T(8,128)S(1)} %outer.1), channel_id=1, replica_groups={{0,2,4,6,8,10,12,14,16,18,20,22,24,26,28,30},{1,3,5,7,9,11,13,15,17,19,..., dimensions={0} | all-to-all | bytes 262144 | tf_op jit(solution)/shard_map/all_to_all | solution.py:760
  36.4 0.2 collective-permute-start.1
  36.6 0.1 pad_add_fusion.place
  36.7 1.1 %collective-permute-done.1 = f32[16,2,8,128]{3,2,1,0:T(8,128)S(1)} collective-permute-done((f32[16,2,8,128]{3,2,1,0:T(8,128)S(1)}, f32[16,2,8,128]{3,2,1,0:T(8,128)S(1)}, u32[]{:S(2)}, u32[]{:S(2)}) %collective-permute-start.1) | collective-permute-done | bytes 131104 | tf_op jit(solution)/shard_map/ppermute | solution.py:763
  37.7 1.6 %factor.1 = (f32[4,1,256]{2,1,0:T(1,128)}, f32[8,8]{1,0:T(8,128)}) custom-call(s32[2]{0:T(128)S(1)} %pad_add_fusion.place, f32[256,128]{1,0:T(8,128)S(1)} %bitcast.6, f32[256,128]{1,0:T(8,128)S(1)} %bitcast.7), custom_call_target="tpu_custom_call" | custom-call | tf_op jit(solution)/shard_map/factor/pallas_call | solution.py:773
Async XLA Ops:
  0.6 4.9 %copy-start.1 = (s32[8,32,512]{2,1,0:T(8,128)S(1)}, s32[8,32,512]{2,1,0:T(8,128)}, u32[]{:S(2)}) copy-start(s32[8,32,512]{2,1,0:T(8,128)} %sites_in.3) | copy-start | bytes 1572868
  0.6 4.9 %copy-start = (f32[8,32,512]{2,1,0:T(8,128)S(1)}, f32[8,32,512]{2,1,0:T(8,128)}, u32[]{:S(2)}) copy-start(f32[8,32,512]{2,1,0:T(8,128)} %background_in.3) | copy-start | bytes 1572868
  4.1 7.8 %collective-permute-start = (f32[180,8,128]{2,1,0:T(8,128)}, f32[180,8,128]{2,1,0:T(8,128)S(1)}, u32[]{:S(2)}, u32[]{:S(2)}) collective-permute-start(f32[180,8,128]{2,1,0:T(8,128)} %packet.1), channel_id=1, source_target_pairs={{1,0},{2,1},{3,2},{4,3},{5,4},{6,5},{7,6},{8,7},{9,8},{10,9},{11,1... | collective-permute-start | bytes 2211848 | tf_op jit(solution)/shard_map/ppermute | solution.py:719
  5.4 0.7 %copy-start.2 = (f32[4,1,256]{2,1,0:T(1,128)S(1)}, f32[4,1,256]{2,1,0:T(1,128)}, u32[]{:S(2)}) copy-start(f32[4,1,256]{2,1,0:T(1,128)} %dirs_in.3) | copy-start | bytes 12292
  5.4 0.7 %copy-start.3 = (f32[1,256]{1,0:T(1,128)S(1)}, f32[1,256]{1,0:T(1,128)}, u32[]{:S(2)}) copy-start(f32[1,256]{1,0:T(1,128)} %log_param_in.3) | copy-start | bytes 3076
  5.5 0.7 %copy-start.4 = (f32[4]{0:T(128)S(1)}, f32[4]{0:T(128)}, u32[]{:S(2)}) copy-start(f32[4]{0:T(128)} %density.3) | copy-start | bytes 52
  36.4 1.3 %collective-permute-start.1 = (f32[16,2,8,128]{3,2,1,0:T(8,128)S(1)}, f32[16,2,8,128]{3,2,1,0:T(8,128)S(1)}, u32[]{:S(2)}, u32[]{:S(2)}) collective-permute-start(f32[16,2,8,128]{3,2,1,0:T(8,128)S(1)} %all_to_all.5), channel_id=1, source_target_pairs={{0,1},{1,0},{2,3},{3,2},{4,5},{5,4},{6,7},{7,6},{8,9},{9,8},{10,11... | collective-permute-start | bytes 393224 | tf_op jit(solution)/shard_map/ppermute | solution.py:763

commit v2 on v1

--- a/solution.py
+++ b/solution.py
@@ -40,15 +40,28 @@
     return jnp.dot(a, b, preferred_element_type=jnp.float32)
 
 
-def interleave(background, sites, order, bg, site):
-    count = background.shape[0]
-    parts = list(parts_of(background)) + [sites.astype(jnp.bfloat16)]
+def interleave(exact, small, order):
+    parts = [part for x in exact for part in parts_of(x)] + [x.astype(jnp.bfloat16) for x in small]
     placed = bf16_dot(jnp.concatenate(parts, axis=0), order[...])
-    for k in range(bg.shape[0]):
-        columns = placed[:, k * LANES : (k + 1) * LANES]
-        both = columns[:count] + columns[count : 2 * count]
-        bg[k] = both + columns[2 * count : 3 * count]
-        site[k] = columns[3 * count :]
+    results, at = [], 0
+    for x in exact:
+        count = x.shape[0]
+        first, second, third = [placed[at + n * count : at + (n + 1) * count] for n in range(3)]
+        results.append((first + second) + third)
+        at += 3 * count
+    for x in small:
+        results.append(placed[at : at + x.shape[0]])
+        at += x.shape[0]
+    return results
+
+
+def keep(placed, kept):
+    for k in range(kept.shape[0]):
+        kept[k] = placed[:, k * LANES : (k + 1) * LANES]
+
+
+def flat(planes):
+    return planes.reshape((planes.shape[0] * planes.shape[1], planes.shape[2]))
 
 
 def cell_matrix(chunks, turned=False):
@@ -99,45 +112,38 @@
     return [spread[8 * n : 8 * n + 8, :] for n in range(probes + 1)]
 
 
-def weights_and_sources(density, scale, background, sites, planes, order, bg, site, store):
-    first, count = planes
-    rows, columns = background.shape[1:]
-    chunks, folds = columns // LANES, rows // 8
-    at = pl.ds(first, count)
-    cells = (count * rows, columns)
-    interleave(
-        background[at].reshape(cells),
-        sites[at].reshape(cells).astype(jnp.float32),
-        order,
-        bg,
-        site,
-    )
-    for z in range(count):
-        for r in range(folds):
-            for k in range(chunks):
-                row = pl.ds(z * rows + r, 8, stride=folds)
-                kind = site[k, row, :]
-                trap = jnp.full((8, LANES), density[density.shape[0] - 1])
-                for n in range(density.shape[0] - 2, -1, -1):
-                    trap = jnp.where(kind == float(n), density[n], trap)
-                trap = trap * scale
-                weight = (1.0 / STEP - 6.0) - trap
-                store(first + z, r * chunks + k, weight, -STEP * trap * bg[k, row, :])
+def tile_rows(z, r, rows, folds):
+    return pl.ds(z * rows + r, 8, stride=folds)
+
+
+def trap_of(density, kind):
+    trap = jnp.full((8, LANES), density[density.shape[0] - 1])
+    for n in range(density.shape[0] - 2, -1, -1):
+        trap = jnp.where(kind == float(n), density[n], trap)
+    return trap
+
+
+def weight_of(trap):
+    return (1.0 / STEP - 6.0) - trap
+
+
+def source_of(trap, background):
+    return -STEP * trap * background
 
 
 def packet_kernel(
     density, background_in, sites_in, log_param_in, dirs_in, packet,
     background, sites, log_param, dirs, order, bg, site, made, sems, out_sems,
 ):
-    rows, columns = background.shape[1:]
+    count, rows, columns = sites.shape
     chunks, folds = columns // LANES, rows // 8
     tiles = chunks * folds
     probes = dirs.shape[0]
     pairs = [
         (log_param_in, log_param),
         (dirs_in, dirs),
-        (background_in.at[pl.ds(0, 2 * HALO)], background),
-        (sites_in.at[pl.ds(0, 2 * HALO)], sites),
+        (background_in.at[pl.ds(count - 1, 1)], background),
+        (sites_in.at[pl.ds(0, count)], sites),
     ]
     copies = [pltpu.make_async_copy(a, b, sems.at[n]) for n, (a, b) in enumerate(pairs)]
     for copy in copies:
@@ -148,33 +154,35 @@
     spread = spread_cells(dirs, log_param, folds, chunks)
     for p in range(probes):
         made[p] = spread[p]
-
-    first_weight = probes + 2 * HALO * tiles
-    ranges = {
-        HALO - 1: [(0, probes + HALO * tiles), (first_weight, HALO * tiles)],
-        2 * HALO - 1: [
-            (probes + HALO * tiles, HALO * tiles),
-            (first_weight + HALO * tiles, (HALO - 1) * tiles),
-        ],
-    }
-    sent = []
-
-    def store(z, t, weight, source):
-        made[probes + z * tiles + t] = source
-        if z < 2 * HALO - 1:
-            made[probes + (2 * HALO + z) * tiles + t] = weight
-        if t == tiles - 1:
-            for start, length in ranges.get(z, []):
-                at = pl.ds(start, length)
-                copy = pltpu.make_async_copy(made.at[at], packet.at[at], out_sems.at[len(sent)])
-                copy.start()
-                sent.append(copy)
-
     copies[2].wait()
     copies[3].wait()
-    weights_and_sources(
-        density, spread[probes], background, sites, (0, 2 * HALO), order, bg, site, store
-    )
+    placed = interleave([flat(background[...])], [flat(sites[...]).astype(jnp.float32)], order)
+    keep(placed[0], bg)
+    keep(placed[1], site)
+    sent = []
+
+    def send(start, stop):
+        at = pl.ds(start, stop - start)
+        copy = pltpu.make_async_copy(made.at[at], packet.at[at], out_sems.at[len(sent)])
+        copy.start()
+        sent.append(copy)
+
+    first = probes + tiles
+    middle = first + (count - 1) // 2 * tiles
+    for z in range(count):
+        for r in range(folds):
+            for k in range(chunks):
+                t = r * chunks + k
+                trap = trap_of(density, site[k, tile_rows(z, r, rows, folds), :]) * spread[probes]
+                if z < count - 1:
+                    made[first + z * tiles + t] = trap
+                else:
+                    made[probes + t] = source_of(trap, bg[k, tile_rows(0, r, rows, folds), :])
+        if z == (count - 1) // 2 - 1:
+            send(first, middle)
+        elif z == count - 2:
+            send(middle, first + (count - 1) * tiles)
+    send(0, first)
     for copy in sent:
         copy.wait()
 
@@ -376,9 +384,9 @@
 
 
 def inner_kernel(
-    edge, density, background_in, sites_in, log_param_in, dirs_in,
-    coef, src, wide, kept, sums,
-    background, sites, log_param, dirs, order, bg, site, even, odd, sems,
+    edge, density, background_in, sites_in, log_param_in, dirs_in, beyond,
+    coef, src, wide, kept, sums, next_bg,
+    background, sites, log_param, dirs, order, bg, far, site, even, odd, sems,
 ):
     planes, rows, columns = background.shape
     chunks, folds = columns // LANES, rows // 8
@@ -405,13 +413,21 @@
     for p in range(probes):
         wide[p] = spread[p]
 
-    def store(z, t, weight, source):
-        coef[z * tiles + t] = weight
-        src[z * tiles + t] = source
-
-    weights_and_sources(
-        density, spread[probes], background, sites, (0, planes), order, bg, site, store
+    placed = interleave(
+        [flat(background[...]), flat(beyond[...])], [flat(sites[...]).astype(jnp.float32)], order
     )
+    for x, scratch in zip(placed, (bg, far, site)):
+        keep(x, scratch)
+    for r in range(folds):
+        for k in range(chunks):
+            t = r * chunks + k
+            for z in range(planes):
+                at = tile_rows(z, r, rows, folds)
+                trap = trap_of(density, site[k, at, :]) * spread[probes]
+                coef[z * tiles + t] = weight_of(trap)
+                src[z * tiles + t] = source_of(trap, bg[k, at, :])
+            for z in range(beyond.shape[0]):
+                next_bg[z * tiles + t] = far[k, tile_rows(z, r, rows, folds), :]
     at_low = edge[0] != 0
 
     def low(z):
@@ -433,7 +449,7 @@
 
 
 def outer_kernel(
-    chunks, folds, edge, own_coef, own_src, own_wide, kept, own_sums, packet, out,
+    chunks, folds, edge, own_coef, own_src, own_wide, kept, own_sums, next_bg, packet, out,
     coef, src, even, odd,
 ):
     tiles = chunks * folds
@@ -455,8 +471,17 @@
     own = (last - HALO) * tiles
     copy(own_src, own, src, own, planes - last + HALO)
     copy(own_coef, own, coef, own, planes - last + HALO)
-    copy(packet, probes, src, halo, 2 * HALO)
-    copy(packet, probes + 2 * HALO * tiles, coef, halo, 2 * HALO - 1)
+
+    def beyond_plane(n, carry):
+        for t in range(tiles):
+            at = n * tiles + t
+            trap = packet[probes + tiles + at]
+            coef[halo + at] = weight_of(trap)
+            src[halo + at] = source_of(trap, next_bg[at])
+        return carry
+
+    lax.fori_loop(0, 2 * HALO - 1, beyond_plane, 0)
+    copy(packet, probes, src, (total - 1) * tiles, 1)
     steps.clear(even, odd)
     for p in range(probes):
         for t in range(tiles):
@@ -691,10 +716,10 @@
     def copies(count):
         return pltpu.SemaphoreType.DMA((count,))
 
-    def inputs(held):
+    def inputs(held, sites):
         return [
             pltpu.VMEM((held, rows, columns), jnp.float32),
-            pltpu.VMEM((held, rows, columns), jnp.int32),
+            pltpu.VMEM((sites, rows, columns), jnp.int32),
             pltpu.VMEM(log_param.shape, jnp.float32),
             pltpu.VMEM(probe_dirs.shape, jnp.float32),
             pltpu.VMEM((columns, columns), jnp.bfloat16),
@@ -703,22 +728,22 @@
     def rows_of(held):
         return pltpu.VMEM((chunks, held * rows, LANES), jnp.float32)
 
-    size = probes + (4 * HALO - 1) * tiles
+    down = [(i + 1, i) for i in range(slabs - 1)]
+    beyond = lax.ppermute(background[: 2 * HALO - 1], "space", down)
+    size = probes + 2 * HALO * tiles
     packet = pl.pallas_call(
         packet_kernel,
         out_shape=shape(size),
         in_specs=[smem] + [anywhere] * 4,
         out_specs=anywhere,
-        scratch_shapes=inputs(2 * HALO)
-        + [rows_of(2 * HALO), rows_of(2 * HALO), scratch(size), copies(4), copies(4)],
+        scratch_shapes=inputs(1, 2 * HALO)
+        + [rows_of(1), rows_of(2 * HALO), scratch(size), copies(4), copies(3)],
         compiler_params=params,
         name="packet",
     )(trap_density, background, site_class, log_param, probe_dirs)
-
-    down = [(i + 1, i) for i in range(slabs - 1)]
     next_packet = lax.ppermute(packet, "space", down)
     edge = jnp.stack([at_space > 0, at_space < slabs - 1]).astype(jnp.int32)
-    own_coef, own_src, wide, kept, sums = pl.pallas_call(
+    own_coef, own_src, wide, kept, sums, next_bg = pl.pallas_call(
         inner_kernel,
         out_shape=(
             shape(planes * tiles),
@@ -726,23 +751,24 @@
             shape(probes),
             shape(4, probes, tiles),
             shape(probes),
+            shape((2 * HALO - 1) * tiles),
         ),
-        in_specs=[smem, smem] + [anywhere] * 4,
-        out_specs=(vmem,) * 5,
-        scratch_shapes=inputs(planes)
-        + [rows_of(planes), rows_of(planes)]
+        in_specs=[smem, smem] + [anywhere] * 4 + [vmem],
+        out_specs=(vmem,) * 6,
+        scratch_shapes=inputs(planes, planes)
+        + [rows_of(planes), rows_of(2 * HALO - 1), rows_of(planes)]
         + [scratch(planes + 1, probes, tiles)] * 2
         + [copies(4)],
         compiler_params=pltpu.CompilerParams(vmem_limit_bytes=28 * 2**20),
         cost_estimate=pl.CostEstimate(flops=10**9, bytes_accessed=2**24, transcendentals=256),
         name="inner",
-    )(edge, trap_density, background, site_class, log_param, probe_dirs)
+    )(edge, trap_density, background, site_class, log_param, probe_dirs, beyond)
 
     pieces = probes * cells // LANES
     images = pl.pallas_call(
         functools.partial(outer_kernel, chunks, folds),
         out_shape=jax.ShapeDtypeStruct((groups * slabs // 2, 2, pieces, LANES), jnp.float32),
-        in_specs=[smem] + [vmem] * 6,
+        in_specs=[smem] + [vmem] * 7,
         out_specs=vmem,
         scratch_shapes=[
             scratch(total * tiles),
@@ -752,7 +778,7 @@
         ],
         compiler_params=pltpu.CompilerParams(vmem_limit_bytes=28 * 2**20),
         name="outer",
-    )(edge, own_coef, own_src, wide, kept, sums, next_packet)
+    )(edge, own_coef, own_src, wide, kept, sums, next_bg, next_packet)
 
     same = [
         [g * slabs + z for g in range(groups) for z in range(parity, slabs, 2)] for parity in (0, 1)

time: 39.5 us -> 39.1 us (0.990)
  blocking collectives: 19.8 us -> 17.2 us
  starting transfers between devices: 1.49 us -> 2.97 us
  local copies, waits for them, and re-layouts: 0.6 us -> 1.59 us
    all_to_all x1, blocking collectives: 19.8 us -> 17.2 us  [shards(): lax.all_to_all(images, ('probe', 'space'), split_axis=0, concat_axis=0, a...]
    ppermute x0 -> x1, starting transfers between devices: none -> 1.42 us  [shards(): beyond = lax.ppermute(background[:2 * HALO - 1], 'space', down)]
    slice x0 -> x1, local copies, waits for them, and re-layouts: none -> 1 us  [shards(): beyond = lax.ppermute(background[:2 * HALO - 1], 'space', down)]
    pallas_call x1, Pallas kernels: 3.46 us -> 2.84 us  [shards(): pl.pallas_call(packet_kernel, out_shape=shape(size), in_specs=[smem] + [a...]
  transfers between devices with their start and end apart: 2 -> 3, of which waited for: 1 -> 1; matrix products, arithmetic and copies ran while one was open for 0% -> 0% of each run, Pallas kernels for 15% -> 23%
where the time goes in v2:
time: 39.1 us; the launch traced here: 38.8 us
  blocking collectives  17.2 us (44%)
  Pallas kernels  15.2 us (39%)
  starting transfers between devices  2.97 us (8%)
  local copies, waits for them, and re-layouts  1.59 us (4%)
  waiting for transfers between devices  1.02 us (3%)
  between operations  0.74 us (2%)
    all_to_all x1, blocking collectives, shards(): lax.all_to_all(images, ('probe', 'space'), split_axis=0, concat_axis=0, a...  17.2 us
    pallas_call x1, Pallas kernels, shards(): pl.pallas_call(inner_kernel, out_shape=(shape(planes * tiles), shape((pla...  6.04 us
    pallas_call x1, Pallas kernels, shards(): pl.pallas_call(functools.partial(outer_kernel, chunks, folds), out_shape=...  4.74 us
    pallas_call x1, Pallas kernels, shards(): pl.pallas_call(packet_kernel, out_shape=shape(size), in_specs=[smem] + [a...  2.84 us
    pallas_call x1, Pallas kernels, shards(): pl.pallas_call(functools.partial(register_kernel, groups, slabs, probes),...  1.57 us
    ppermute x1, starting transfers between devices, shards(): beyond = lax.ppermute(background[:2 * HALO - 1], 'space', down)  1.42 us
    ppermute x1, starting transfers between devices, shards(): next_packet = lax.ppermute(packet, 'space', down)  1.29 us
    ppermute x1, waiting for transfers between devices, shards(): other = lax.ppermute(mine, 'space', [(z, z ^ 1) for z in range(slabs)])  1.01 us
  transfers between devices with their start and end apart: 3, of which 1 were waited for; matrix products, arithmetic and copies ran while one was open for 0% of the time, Pallas kernels for 23%

profile of v2, /device:TPU:0, one launch (start us, length us, event | category | flops | bytes accessed | tf_op | source)
XLA Modules:
  0.0 38.8 jit_solution(6304637269395731536)
XLA Ops:
  0.6 1.0 %slice.3 = f32[5,32,512]{2,1,0:T(8,128)S(1)} slice(f32[8,32,512]{2,1,0:T(8,128)} %background_in.3), slice={[0:5], [0:32], [0:512]} | slice | bytes 655360 | tf_op jit(solution)/shard_map/slice | solution.py:732
  1.6 0.0 copy-start
  1.6 0.0 copy-start.1
  1.7 1.4 %collective-permute-start = (f32[5,32,512]{2,1,0:T(8,128)S(1)}, f32[5,32,512]{2,1,0:T(8,128)S(1)}, u32[]{:S(2)}, u32[]{:S(2)}) collective-permute-start(f32[5,32,512]{2,1,0:T(8,128)S(1)} %slice.3), channel_id=1, source_target_pairs={{1,0},{2,1},{3,2},{4,3},{5,4},{6,5},{7,6},{8,7},{9,8},{10,9},{11,1... | collective-permute-start | bytes 983048 | tf_op jit(solution)/shard_map/ppermute | solution.py:732
  3.1 2.8 %packet.1 = f32[100,8,128]{2,1,0:T(8,128)} custom-call(f32[4]{0:T(128)} %density.3, f32[8,32,512]{2,1,0:T(8,128)} %background_in.3, s32[8,32,512]{2,1,0:T(8,128)} %sites_in.3, f32[1,256]{1,0:T(1,128)} %log_param_in.3, f32[4,1,256]{2,1,0:T(1,128)} %dirs_in.3), custom_call_target="tpu_custom_call" | custom-call | tf_op jit(solution)/shard_map/packet/pallas_call | solution.py:734
  5.9 1.3 %collective-permute-start.1 = (f32[100,8,128]{2,1,0:T(8,128)}, f32[100,8,128]{2,1,0:T(8,128)S(1)}, u32[]{:S(2)}, u32[]{:S(2)}) collective-permute-start(f32[100,8,128]{2,1,0:T(8,128)} %packet.1), channel_id=1, source_target_pairs={{1,0},{2,1},{3,2},{4,3},{5,4},{6,5},{7,6},{8,7},{9,8},{10,9},{11,1... | collective-permute-start | bytes 1228808 | tf_op jit(solution)/shard_map/ppermute | solution.py:744
  7.2 0.0 copy-start.2
  7.3 0.0 copy-start.3
  7.3 0.0 copy-start.4
  7.3 0.1 add_convert_fusion.edge
  7.4 0.0 collective-permute-done.beyond
  7.4 0.0 copy-done
  7.4 0.0 copy-done.1
  7.4 0.6 %copy-done.2 = f32[4,1,256]{2,1,0:T(1,128)S(1)} copy-done((f32[4,1,256]{2,1,0:T(1,128)S(1)}, f32[4,1,256]{2,1,0:T(1,128)}, u32[]{:S(2)}) %copy-start.2) | copy-done | bytes 4120
  7.9 0.0 copy-done.3
  7.9 0.0 copy-done.4
  7.9 6.0 %inner.1 = (f32[128,8,128]{2,1,0:T(8,128)S(1)}, f32[144,8,128]{2,1,0:T(8,128)S(1)}, f32[4,8,128]{2,1,0:T(8,128)S(1)}, f32[4,4,16,8,128]{4,3,2,1,0:T(8,128)S(1)},...) custom-call(s32[2]{0:T(128)S(1)} %add_convert_fusion.edge, f32[4]{0:T(128)S(1)} %copy-done.4, ...), custom_call_target="tpu_custom_call" | custom-call | flops 1000000000 | bytes 16777216 | tf_op jit(solution)/shard_map/inner/pallas_call | solution.py:746
  14.0 0.0 collective-permute-done.1.packet
  14.0 4.7 %outer.1 = f32[16,2,8,128]{3,2,1,0:T(8,128)S(1)} custom-call(s32[2]{0:T(128)S(1)} %add_convert_fusion.edge, f32[128,8,128]{2,1,0:T(8,128)S(1)} %get-tuple-element.8.own_coef, f32[144,8,128]{2,1,0:T(8,128)S(1)} %get-tuple-element.9.own_src, f32[4,8,128]{2,1,0:T(8,128)S(1)} %get-tuple-element.10.own_wide, f32[4,4,16,8,128]{4,3,2,1,0:T(8,128)S(1)} %get-tuple-element.11.kept, ...), custom_call_target="tpu_custom_call" | custom-call | tf_op jit(solution)/shard_map/outer/pallas_call | solution.py:768
  18.8 17.2 %all_to_all.5 = f32[16,2,8,128]{3,2,1,0:T(8,128)S(1)} all-to-all(f32[16,2,8,128]{3,2,1,0:T(8,128)S(1)} %outer.1), channel_id=1, replica_groups={{0,2,4,6,8,10,12,14,16,18,20,22,24,26,28,30},{1,3,5,7,9,11,13,15,17,19,..., dimensions={0} | all-to-all | bytes 262144 | tf_op jit(solution)/shard_map/all_to_all | solution.py:786
  35.9 0.3 collective-permute-start.2
  36.2 0.1 pad_add_fusion.place
  36.3 1.0 %collective-permute-done.2 = f32[16,2,8,128]{3,2,1,0:T(8,128)S(1)} collective-permute-done((f32[16,2,8,128]{3,2,1,0:T(8,128)S(1)}, f32[16,2,8,128]{3,2,1,0:T(8,128)S(1)}, u32[]{:S(2)}, u32[]{:S(2)}) %collective-permute-start.2) | collective-permute-done | bytes 131104 | tf_op jit(solution)/shard_map/ppermute | solution.py:789
  37.3 1.6 %factor.1 = (f32[4,1,256]{2,1,0:T(1,128)}, f32[8,8]{1,0:T(8,128)}) custom-call(s32[2]{0:T(128)S(1)} %pad_add_fusion.place, f32[256,128]{1,0:T(8,128)S(1)} %bitcast.6, f32[256,128]{1,0:T(8,128)S(1)} %bitcast.7), custom_call_target="tpu_custom_call" | custom-call | tf_op jit(solution)/shard_map/factor/pallas_call | solution.py:799
Async XLA Ops:
  1.6 5.7 %copy-start = (f32[8,32,512]{2,1,0:T(8,128)S(1)}, f32[8,32,512]{2,1,0:T(8,128)}, u32[]{:S(2)}) copy-start(f32[8,32,512]{2,1,0:T(8,128)} %background_in.3) | copy-start | bytes 1572868
  1.6 5.7 %copy-start.1 = (s32[8,32,512]{2,1,0:T(8,128)S(1)}, s32[8,32,512]{2,1,0:T(8,128)}, u32[]{:S(2)}) copy-start(s32[8,32,512]{2,1,0:T(8,128)} %sites_in.3) | copy-start | bytes 1572868
  1.7 5.7 %collective-permute-start = (f32[5,32,512]{2,1,0:T(8,128)S(1)}, f32[5,32,512]{2,1,0:T(8,128)S(1)}, u32[]{:S(2)}, u32[]{:S(2)}) collective-permute-start(f32[5,32,512]{2,1,0:T(8,128)S(1)} %slice.3), channel_id=1, source_target_pairs={{1,0},{2,1},{3,2},{4,3},{5,4},{6,5},{7,6},{8,7},{9,8},{10,9},{11,1... | collective-permute-start | bytes 983048 | tf_op jit(solution)/shard_map/ppermute | solution.py:732
  5.9 8.1 %collective-permute-start.1 = (f32[100,8,128]{2,1,0:T(8,128)}, f32[100,8,128]{2,1,0:T(8,128)S(1)}, u32[]{:S(2)}, u32[]{:S(2)}) collective-permute-start(f32[100,8,128]{2,1,0:T(8,128)} %packet.1), channel_id=1, source_target_pairs={{1,0},{2,1},{3,2},{4,3},{5,4},{6,5},{7,6},{8,7},{9,8},{10,9},{11,1... | collective-permute-start | bytes 1228808 | tf_op jit(solution)/shard_map/ppermute | solution.py:744
  7.2 0.7 %copy-start.2 = (f32[4,1,256]{2,1,0:T(1,128)S(1)}, f32[4,1,256]{2,1,0:T(1,128)}, u32[]{:S(2)}) copy-start(f32[4,1,256]{2,1,0:T(1,128)} %dirs_in.3) | copy-start | bytes 12292
  7.3 0.7 %copy-start.3 = (f32[1,256]{1,0:T(1,128)S(1)}, f32[1,256]{1,0:T(1,128)}, u32[]{:S(2)}) copy-start(f32[1,256]{1,0:T(1,128)} %log_param_in.3) | copy-start | bytes 3076
  7.3 0.7 %copy-start.4 = (f32[4]{0:T(128)S(1)}, f32[4]{0:T(128)}, u32[]{:S(2)}) copy-start(f32[4]{0:T(128)} %density.3) | copy-start | bytes 52
  35.9 1.3 %collective-permute-start.2 = (f32[16,2,8,128]{3,2,1,0:T(8,128)S(1)}, f32[16,2,8,128]{3,2,1,0:T(8,128)S(1)}, u32[]{:S(2)}, u32[]{:S(2)}) collective-permute-start(f32[16,2,8,128]{3,2,1,0:T(8,128)S(1)} %all_to_all.5), channel_id=1, source_target_pairs={{0,1},{1,0},{2,3},{3,2},{4,5},{5,4},{6,7},{7,6},{8,9},{9,8},{10,11... | collective-permute-start | bytes 393224 | tf_op jit(solution)/shard_map/ppermute | solution.py:789

commit v3 on v2

--- a/solution.py
+++ b/solution.py
@@ -638,7 +638,8 @@
     return factor, rows
 
 
-def register_kernel(groups, slabs, probes, place, mine, other, q_out, lower_out, q_ref):
+def register_kernel(turns, slabs, probes, place, mine, other, q_out, lower_out, q_ref):
+    groups = len(turns)
     halves = q_out.shape[2] // LANES
     pieces = probes * halves
     step = 2 * pieces
@@ -646,34 +647,32 @@
     odd = jnp.broadcast_to(place[1] % 2, (8, LANES)) == 1
 
     def load(at):
-        at = pl.ds(at, 8, stride=step)
+        at = pl.ds(at, 8, stride=groups * step)
         one, two = mine[at, :], other[at, :]
         return jnp.where(odd, two, one), jnp.where(odd, one, two)
 
     rows = []
-    for g in range(groups):
+    for g, turn in enumerate(turns):
         for p in range(probes):
             row = []
             for h in range(halves):
-                last = None
-                for block in range(slabs // 16):
-                    at = (g * slabs // 2 + 8 * block) * step + p * halves + h
-                    even_own, odd_own = load(at)
-                    even_next, odd_next = load(at + pieces)
-                    before = pltpu.roll(odd_next, 1, 0)
-                    first = 0.0 if last is None else last
-                    last = before
-                    row.append((block, 0, h, even_own + jnp.where(sublane == 0, first, before)))
-                    row.append((block, 1, h, odd_own + even_next))
+                at = g * step + p * halves + h
+                even_own, odd_own = load(at)
+                even_next, odd_next = load(at + pieces)
+                if turn:
+                    even_own, odd_next = pltpu.roll(even_own, turn, 0), pltpu.roll(odd_next, turn + 1, 0)
+                    odd_row = pltpu.roll(odd_own + even_next, turn, 0)
+                else:
+                    odd_next = pltpu.roll(odd_next, 1, 0)
+                    odd_row = odd_own + even_next
+                row += [even_own + jnp.where(sublane == 0, 0.0, odd_next), odd_row]
             rows.append(row)
-    places = [x[:3] for x in rows[0]]
-    rows = [[x[3] for x in row] for row in rows]
     total = slabs * halves * LANES
     factor_one, basis = cholesky(rows, total)
     factor_two, rows = cholesky(basis, total)
     for i, row in enumerate(rows):
-        for (block, parity, h), x in zip(places, row):
-            q_ref[i, h, pl.ds(parity * (slabs // 2) + 8 * block, 8), :] = x
+        for n, x in enumerate(row):
+            q_ref[i, n // 2, pl.ds(n % 2 * 8, 8), :] = x
     own = (place[1] % 2) * (slabs // 2) + place[1] // 2
     for p in range(probes):
         for h in range(halves):
@@ -780,8 +779,15 @@
         name="outer",
     )(edge, own_coef, own_src, wide, kept, sums, next_bg, next_packet)
 
+    half = slabs // 2
+    turns = [half // 2 * (g % 2) for g in range(groups)]
     same = [
-        [g * slabs + z for g in range(groups) for z in range(parity, slabs, 2)] for parity in (0, 1)
+        [
+            g * slabs + 2 * ((n + turns[g]) % half) + parity
+            for n in range(half)
+            for g in range(groups)
+        ]
+        for parity in (0, 1)
     ]
     mine = lax.all_to_all(
         images, ("probe", "space"), split_axis=0, concat_axis=0, axis_index_groups=same, tiled=True
@@ -794,10 +800,10 @@
         jax.ShapeDtypeStruct((count, count), jnp.float32),
     )
     params = pltpu.CompilerParams(vmem_limit_bytes=28 * 2**20)
-    if count <= 8 and slabs % 16 == 0:
+    if count <= 8 and slabs == 16:
         halves = cells // LANES
         return pl.pallas_call(
-            functools.partial(register_kernel, groups, slabs, probes),
+            functools.partial(register_kernel, turns, slabs, probes),
             out_shape=results,
             in_specs=[smem, vmem, vmem],
             out_specs=(vmem, vmem),
@@ -811,7 +817,10 @@
         )
     odd = at_space % 2 == 1
     pairs = [jnp.where(odd, other, mine), jnp.where(odd, mine, other)]
-    pairs = [x.reshape((groups, slabs // 2, 2, probes, cells)) for x in pairs]
+    pairs = [x.reshape((half, groups, 2, probes, cells)) for x in pairs]
+    pairs = [
+        jnp.stack([jnp.roll(x[:, g], turns[g], axis=0) for g in range(groups)]) for x in pairs
+    ]
     every = jnp.stack(pairs, axis=2).reshape((groups, slabs, 2, probes, cells))
     return pl.pallas_call(
         factor_kernel,

time: 39.1 us -> 39.4 us (level)
  no operation moved by 1% of the time
where the time goes in v3:
time: 39.4 us; the launch traced here: 39.1 us
  blocking collectives  17.4 us (44%)
  Pallas kernels  15.2 us (39%)
  starting transfers between devices  3.11 us (8%)
  local copies, waits for them, and re-layouts  1.59 us (4%)
  waiting for transfers between devices  0.92 us (2%)
  between operations  0.74 us (2%)
    all_to_all x1, blocking collectives, shards(): lax.all_to_all(images, ('probe', 'space'), split_axis=0, concat_axis=0, a...  17.4 us
    pallas_call x1, Pallas kernels, shards(): pl.pallas_call(inner_kernel, out_shape=(shape(planes * tiles), shape((pla...  6.04 us
    pallas_call x1, Pallas kernels, shards(): pl.pallas_call(functools.partial(outer_kernel, chunks, folds), out_shape=...  4.74 us
    pallas_call x1, Pallas kernels, shards(): pl.pallas_call(packet_kernel, out_shape=shape(size), in_specs=[smem] + [a...  2.84 us
    pallas_call x1, Pallas kernels, shards(): pl.pallas_call(functools.partial(register_kernel, turns, slabs, probes),...  1.62 us
    ppermute x1, starting transfers between devices, shards(): beyond = lax.ppermute(background[:2 * HALO - 1], 'space', down)  1.42 us
    ppermute x1, starting transfers between devices, shards(): next_packet = lax.ppermute(packet, 'space', down)  1.29 us
    slice x1, local copies, waits for them, and re-layouts, shards(): beyond = lax.ppermute(background[:2 * HALO - 1], 'space', down)  1 us
  transfers between devices with their start and end apart: 3, of which 1 were waited for; matrix products, arithmetic and copies ran while one was open for 0% of the time, Pallas kernels for 23%

profile of v3, /device:TPU:0, one launch (start us, length us, event | category | flops | bytes accessed | tf_op | source)
XLA Modules:
  0.0 39.1 jit_solution(931983963522020804)
XLA Ops:
  0.6 1.0 %slice.3 = f32[5,32,512]{2,1,0:T(8,128)S(1)} slice(f32[8,32,512]{2,1,0:T(8,128)} %background_in.3), slice={[0:5], [0:32], [0:512]} | slice | bytes 655360 | tf_op jit(solution)/shard_map/slice | solution.py:731
  1.6 0.0 copy-start
  1.6 0.0 copy-start.1
  1.7 1.4 %collective-permute-start = (f32[5,32,512]{2,1,0:T(8,128)S(1)}, f32[5,32,512]{2,1,0:T(8,128)S(1)}, u32[]{:S(2)}, u32[]{:S(2)}) collective-permute-start(f32[5,32,512]{2,1,0:T(8,128)S(1)} %slice.3), channel_id=1, source_target_pairs={{1,0},{2,1},{3,2},{4,3},{5,4},{6,5},{7,6},{8,7},{9,8},{10,9},{11,1... | collective-permute-start | bytes 983048 | tf_op jit(solution)/shard_map/ppermute | solution.py:731
  3.1 2.8 %packet.1 = f32[100,8,128]{2,1,0:T(8,128)} custom-call(f32[4]{0:T(128)} %density.3, f32[8,32,512]{2,1,0:T(8,128)} %background_in.3, s32[8,32,512]{2,1,0:T(8,128)} %sites_in.3, f32[1,256]{1,0:T(1,128)} %log_param_in.3, f32[4,1,256]{2,1,0:T(1,128)} %dirs_in.3), custom_call_target="tpu_custom_call" | custom-call | tf_op jit(solution)/shard_map/packet/pallas_call | solution.py:733
  5.9 1.3 %collective-permute-start.1 = (f32[100,8,128]{2,1,0:T(8,128)}, f32[100,8,128]{2,1,0:T(8,128)S(1)}, u32[]{:S(2)}, u32[]{:S(2)}) collective-permute-start(f32[100,8,128]{2,1,0:T(8,128)} %packet.1), channel_id=1, source_target_pairs={{1,0},{2,1},{3,2},{4,3},{5,4},{6,5},{7,6},{8,7},{9,8},{10,9},{11,1... | collective-permute-start | bytes 1228808 | tf_op jit(solution)/shard_map/ppermute | solution.py:743
  7.2 0.0 copy-start.2
  7.3 0.0 copy-start.3
  7.3 0.0 copy-start.4
  7.3 0.1 add_convert_fusion.edge
  7.4 0.0 collective-permute-done.beyond
  7.4 0.0 copy-done
  7.4 0.0 copy-done.1
  7.4 0.6 %copy-done.2 = f32[4,1,256]{2,1,0:T(1,128)S(1)} copy-done((f32[4,1,256]{2,1,0:T(1,128)S(1)}, f32[4,1,256]{2,1,0:T(1,128)}, u32[]{:S(2)}) %copy-start.2) | copy-done | bytes 4120
  7.9 0.0 copy-done.3
  7.9 0.0 copy-done.4
  7.9 6.0 %inner.1 = (f32[128,8,128]{2,1,0:T(8,128)S(1)}, f32[144,8,128]{2,1,0:T(8,128)S(1)}, f32[4,8,128]{2,1,0:T(8,128)S(1)}, f32[4,4,16,8,128]{4,3,2,1,0:T(8,128)S(1)},...) custom-call(s32[2]{0:T(128)S(1)} %add_convert_fusion.edge, f32[4]{0:T(128)S(1)} %copy-done.4, ...), custom_call_target="tpu_custom_call" | custom-call | flops 1000000000 | bytes 16777216 | tf_op jit(solution)/shard_map/inner/pallas_call | solution.py:745
  14.0 0.0 collective-permute-done.1.packet
  14.0 4.7 %outer.1 = f32[16,2,8,128]{3,2,1,0:T(8,128)S(1)} custom-call(s32[2]{0:T(128)S(1)} %add_convert_fusion.edge, f32[128,8,128]{2,1,0:T(8,128)S(1)} %get-tuple-element.8.own_coef, f32[144,8,128]{2,1,0:T(8,128)S(1)} %get-tuple-element.9.own_src, f32[4,8,128]{2,1,0:T(8,128)S(1)} %get-tuple-element.10.own_wide, f32[4,4,16,8,128]{4,3,2,1,0:T(8,128)S(1)} %get-tuple-element.11.kept, ...), custom_call_target="tpu_custom_call" | custom-call | tf_op jit(solution)/shard_map/outer/pallas_call | solution.py:767
  18.8 17.4 %all_to_all.5 = f32[16,2,8,128]{3,2,1,0:T(8,128)S(1)} all-to-all(f32[16,2,8,128]{3,2,1,0:T(8,128)S(1)} %outer.1), channel_id=1, replica_groups={{0,24,2,26,4,28,6,30,8,16,10,18,12,20,14,22},{1,25,3,27,5,29,7,31,9,17,..., dimensions={0} | all-to-all | bytes 262144 | tf_op jit(solution)/shard_map/all_to_all | solution.py:792
  36.1 0.4 %collective-permute-start.2 = (f32[16,2,8,128]{3,2,1,0:T(8,128)S(1)}, f32[16,2,8,128]{3,2,1,0:T(8,128)S(1)}, u32[]{:S(2)}, u32[]{:S(2)}) collective-permute-start(f32[16,2,8,128]{3,2,1,0:T(8,128)S(1)} %all_to_all.5), channel_id=1, source_target_pairs={{0,1},{1,0},{2,3},{3,2},{4,5},{5,4},{6,7},{7,6},{8,9},{9,8},{10,11... | collective-permute-start | bytes 393224 | tf_op jit(solution)/shard_map/ppermute | solution.py:795
  36.5 0.1 pad_add_fusion.place
  36.6 0.9 %collective-permute-done.2 = f32[16,2,8,128]{3,2,1,0:T(8,128)S(1)} collective-permute-done((f32[16,2,8,128]{3,2,1,0:T(8,128)S(1)}, f32[16,2,8,128]{3,2,1,0:T(8,128)S(1)}, u32[]{:S(2)}, u32[]{:S(2)}) %collective-permute-start.2) | collective-permute-done | bytes 131104 | tf_op jit(solution)/shard_map/ppermute | solution.py:795
  37.5 1.6 %factor.1 = (f32[4,1,256]{2,1,0:T(1,128)}, f32[8,8]{1,0:T(8,128)}) custom-call(s32[2]{0:T(128)S(1)} %pad_add_fusion.place, f32[256,128]{1,0:T(8,128)S(1)} %bitcast.6, f32[256,128]{1,0:T(8,128)S(1)} %bitcast.7), custom_call_target="tpu_custom_call" | custom-call | tf_op jit(solution)/shard_map/factor/pallas_call | solution.py:805
Async XLA Ops:
  1.6 5.7 %copy-start = (f32[8,32,512]{2,1,0:T(8,128)S(1)}, f32[8,32,512]{2,1,0:T(8,128)}, u32[]{:S(2)}) copy-start(f32[8,32,512]{2,1,0:T(8,128)} %background_in.3) | copy-start | bytes 1572868
  1.6 5.7 %copy-start.1 = (s32[8,32,512]{2,1,0:T(8,128)S(1)}, s32[8,32,512]{2,1,0:T(8,128)}, u32[]{:S(2)}) copy-start(s32[8,32,512]{2,1,0:T(8,128)} %sites_in.3) | copy-start | bytes 1572868
  1.7 5.7 %collective-permute-start = (f32[5,32,512]{2,1,0:T(8,128)S(1)}, f32[5,32,512]{2,1,0:T(8,128)S(1)}, u32[]{:S(2)}, u32[]{:S(2)}) collective-permute-start(f32[5,32,512]{2,1,0:T(8,128)S(1)} %slice.3), channel_id=1, source_target_pairs={{1,0},{2,1},{3,2},{4,3},{5,4},{6,5},{7,6},{8,7},{9,8},{10,9},{11,1... | collective-permute-start | bytes 983048 | tf_op jit(solution)/shard_map/ppermute | solution.py:731
  5.9 8.1 %collective-permute-start.1 = (f32[100,8,128]{2,1,0:T(8,128)}, f32[100,8,128]{2,1,0:T(8,128)S(1)}, u32[]{:S(2)}, u32[]{:S(2)}) collective-permute-start(f32[100,8,128]{2,1,0:T(8,128)} %packet.1), channel_id=1, source_target_pairs={{1,0},{2,1},{3,2},{4,3},{5,4},{6,5},{7,6},{8,7},{9,8},{10,9},{11,1... | collective-permute-start | bytes 1228808 | tf_op jit(solution)/shard_map/ppermute | solution.py:743
  7.2 0.7 %copy-start.2 = (f32[4,1,256]{2,1,0:T(1,128)S(1)}, f32[4,1,256]{2,1,0:T(1,128)}, u32[]{:S(2)}) copy-start(f32[4,1,256]{2,1,0:T(1,128)} %dirs_in.3) | copy-start | bytes 12292
  7.3 0.7 %copy-start.3 = (f32[1,256]{1,0:T(1,128)S(1)}, f32[1,256]{1,0:T(1,128)}, u32[]{:S(2)}) copy-start(f32[1,256]{1,0:T(1,128)} %log_param_in.3) | copy-start | bytes 3076
  7.3 0.7 %copy-start.4 = (f32[4]{0:T(128)S(1)}, f32[4]{0:T(128)}, u32[]{:S(2)}) copy-start(f32[4]{0:T(128)} %density.3) | copy-start | bytes 52
  36.1 1.4 %collective-permute-start.2 = (f32[16,2,8,128]{3,2,1,0:T(8,128)S(1)}, f32[16,2,8,128]{3,2,1,0:T(8,128)S(1)}, u32[]{:S(2)}, u32[]{:S(2)}) collective-permute-start(f32[16,2,8,128]{3,2,1,0:T(8,128)S(1)} %all_to_all.5), channel_id=1, source_target_pairs={{0,1},{1,0},{2,3},{3,2},{4,5},{5,4},{6,7},{7,6},{8,9},{9,8},{10,11... | collective-permute-start | bytes 393224 | tf_op jit(solution)/shard_map/ppermute | solution.py:795

commit v4 on v2

--- a/solution.py
+++ b/solution.py
@@ -195,12 +195,24 @@
         self.lane = lax.broadcasted_iota(jnp.int32, (8, LANES), 1)
         self.sublane = lax.broadcasted_iota(jnp.int32, (8, LANES), 0)
 
+    def rows(self, t, moved=0):
+        r, k = t // self.chunks, t % self.chunks
+        if r in (0, self.folds - 1):
+            return pl.ds(8 + 16 * k + int(r > 0) + 2 * moved, 8, stride=2)
+        return pl.ds(16 + 8 * (self.chunks * (r + 1) + k), 8)
+
+    def load(self, field, plane, p, t, moved=0):
+        return field[plane, p, self.rows(t, moved), :]
+
+    def store(self, field, plane, p, t, value):
+        field[plane, p, self.rows(t), :] = value
+
     def clear(self, *fields):
         nothing = jnp.zeros((8, LANES), jnp.float32)
         for t in range(self.tiles):
             for field in fields:
                 for p in range(self.probes):
-                    field[self.zero_plane, p, t] = nothing
+                    self.store(field, self.zero_plane, p, t, nothing)
 
     def from_left(self, x):
         return jnp.where(self.lane == 0, 0.0, pltpu.roll(x, 1, 1))
@@ -248,7 +260,7 @@
                         result = same * own[p]
                         for value, factor in outer:
                             result = result + value * factor[p]
-                        to[z, p, t] = result
+                        self.store(to, z, p, t, result)
             return carry
 
         return body
@@ -262,7 +274,9 @@
 
         down, here, there, up = at(z - 1), at(z), at(z + 1), at(z + 2)
         for p in range(self.probes):
-            pair = [[ref[plane, p, t] for t in range(tiles)] for plane in (here, there)]
+            pair = [
+                [self.load(ref, plane, p, t) for t in range(tiles)] for plane in (here, there)
+            ]
             for r in range(folds):
                 for k in range(chunks):
                     t = r * chunks + k
@@ -275,12 +289,14 @@
                         if r:
                             before = value[t - chunks]
                         else:
-                            before = self.from_before(value[t + tiles - chunks])
+                            before = self.load(ref, (here, there)[n], p, t + tiles - chunks, -1)
+                            before = jnp.where(self.sublane == 0, 0.0, before)
                         if r + 1 < folds:
                             after = value[t + chunks]
                         else:
-                            after = self.from_after(value[t + chunks - tiles])
-                        above = pair[1 - n][t] + (ref[up, p, t] if n else ref[down, p, t])
+                            after = self.load(ref, (here, there)[n], p, t + chunks - tiles, 1)
+                            after = jnp.where(self.sublane == 7, 0.0, after)
+                        above = pair[1 - n][t] + self.load(ref, up if n else down, p, t)
                         weight = self.coef[(z + n) * tiles + t]
                         if extra:
                             weight = weight + extra
@@ -292,7 +308,7 @@
 
         def body(n, carry):
             def emit(z, p, t, result):
-                to[z, p, t] = result
+                self.store(to, z, p, t, result)
 
             self.stencil(ref, valid, jnp.minimum(start + 2 * n, stop - 2), emit, extra)
             return carry
@@ -305,7 +321,7 @@
         def move(a, b):
             for p in range(self.probes):
                 for t in range(self.tiles):
-                    to[b, p, t] = ref[a, p, t]
+                    self.store(to, b, p, t, self.load(ref, a, p, t))
 
         pl.when(at_low)(lambda: move(first, first - 1))
         pl.when(at_high)(lambda: move(stop - 1, stop))
@@ -350,8 +366,8 @@
                         same = same + value
                 scaled = s[t] * (1.0 / STEP**2)
                 for p in range(self.probes):
-                    value = m[here, p, t]
-                    carry[p][0] = carry[p][0] + (same * value + scaled * u[kept, p, t])
+                    value = self.load(m, here, p, t)
+                    carry[p][0] = carry[p][0] + (same * value + scaled * self.load(u, kept, p, t))
                     for n, factor in moved:
                         carry[p][n] = carry[p][n] + factor * value
             return tuple(tuple(c) for c in carry)
@@ -439,7 +455,7 @@
     for n, (ref, z) in enumerate(((odd, last), (odd, last + 1), (even, last - 1), (even, last))):
         for p in range(probes):
             for t in range(tiles):
-                kept[n, p, t] = ref[z, p, t]
+                kept[n, p, t] = steps.load(ref, z, p, t)
     mine = (low(HALO), last)
     steps.step(even, odd, (low(2), last + 1), mine)
     by_one, by_two = steps.after_tangent(odd, even, mine, at_low, True)
@@ -485,10 +501,10 @@
     steps.clear(even, odd)
     for p in range(probes):
         for t in range(tiles):
-            odd[last, p, t] = kept[0, p, t]
-            odd[last + 1, p, t] = kept[1, p, t]
-            even[last - 1, p, t] = kept[2, p, t]
-            even[last, p, t] = kept[3, p, t]
+            steps.store(odd, last, p, t, kept[0, p, t])
+            steps.store(odd, last + 1, p, t, kept[1, p, t])
+            steps.store(even, last - 1, p, t, kept[2, p, t])
+            steps.store(even, last, p, t, kept[3, p, t])
 
     at_high = edge[1] != 0
 
@@ -713,6 +729,9 @@
     def scratch(*dims):
         return pltpu.VMEM(dims + tile, jnp.float32)
 
+    def field_of(planes):
+        return pltpu.VMEM((planes + 1, probes, 8 * tiles + 16, LANES), jnp.float32)
+
     def copies(count):
         return pltpu.SemaphoreType.DMA((count,))
 
@@ -757,7 +776,7 @@
         out_specs=(vmem,) * 6,
         scratch_shapes=inputs(planes, planes)
         + [rows_of(planes), rows_of(2 * HALO - 1), rows_of(planes)]
-        + [scratch(planes + 1, probes, tiles)] * 2
+        + [field_of(planes)] * 2
         + [copies(4)],
         compiler_params=pltpu.CompilerParams(vmem_limit_bytes=28 * 2**20),
         cost_estimate=pl.CostEstimate(flops=10**9, bytes_accessed=2**24, transcendentals=256),
@@ -773,8 +792,8 @@
         scratch_shapes=[
             scratch(total * tiles),
             scratch(total * tiles),
-            scratch(total + 1, probes, tiles),
-            scratch(total + 1, probes, tiles),
+            field_of(total),
+            field_of(total),
         ],
         compiler_params=pltpu.CompilerParams(vmem_limit_bytes=28 * 2**20),
         name="outer",

time: 39.1 us -> 39.1 us (level)
  no operation moved by 1% of the time
where the time goes in v4:
time: 39.1 us; the launch traced here: 38.8 us
  blocking collectives  17.2 us (44%)
  Pallas kernels  15.1 us (39%)
  starting transfers between devices  2.97 us (8%)
  local copies, waits for them, and re-layouts  1.59 us (4%)
  waiting for transfers between devices  1.02 us (3%)
  between operations  0.74 us (2%)
    all_to_all x1, blocking collectives, shards(): lax.all_to_all(images, ('probe', 'space'), split_axis=0, concat_axis=0, a...  17.2 us
    pallas_call x1, Pallas kernels, shards(): pl.pallas_call(inner_kernel, out_shape=(shape(planes * tiles), shape((pla...  6.02 us
    pallas_call x1, Pallas kernels, shards(): pl.pallas_call(functools.partial(outer_kernel, chunks, folds), out_shape=...  4.72 us
    pallas_call x1, Pallas kernels, shards(): pl.pallas_call(packet_kernel, out_shape=shape(size), in_specs=[smem] + [a...  2.84 us
    pallas_call x1, Pallas kernels, shards(): pl.pallas_call(functools.partial(register_kernel, groups, slabs, probes),...  1.57 us
    ppermute x1, starting transfers between devices, shards(): beyond = lax.ppermute(background[:2 * HALO - 1], 'space', down)  1.42 us
    ppermute x1, starting transfers between devices, shards(): next_packet = lax.ppermute(packet, 'space', down)  1.29 us
    ppermute x1, waiting for transfers between devices, shards(): other = lax.ppermute(mine, 'space', [(z, z ^ 1) for z in range(slabs)])  1.01 us
  transfers between devices with their start and end apart: 3, of which 1 were waited for; matrix products, arithmetic and copies ran while one was open for 0% of the time, Pallas kernels for 23%

profile of v4, /device:TPU:0, one launch (start us, length us, event | category | flops | bytes accessed | tf_op | source)
XLA Modules:
  0.0 38.8 jit_solution(7397761252780087344)
XLA Ops:
  0.6 1.0 %slice.3 = f32[5,32,512]{2,1,0:T(8,128)S(1)} slice(f32[8,32,512]{2,1,0:T(8,128)} %background_in.3), slice={[0:5], [0:32], [0:512]} | slice | bytes 655360 | tf_op jit(solution)/shard_map/slice | solution.py:751
  1.6 0.0 copy-start
  1.6 0.0 copy-start.1
  1.7 1.4 %collective-permute-start = (f32[5,32,512]{2,1,0:T(8,128)S(1)}, f32[5,32,512]{2,1,0:T(8,128)S(1)}, u32[]{:S(2)}, u32[]{:S(2)}) collective-permute-start(f32[5,32,512]{2,1,0:T(8,128)S(1)} %slice.3), channel_id=1, source_target_pairs={{1,0},{2,1},{3,2},{4,3},{5,4},{6,5},{7,6},{8,7},{9,8},{10,9},{11,1... | collective-permute-start | bytes 983048 | tf_op jit(solution)/shard_map/ppermute | solution.py:751
  3.1 2.8 %packet.1 = f32[100,8,128]{2,1,0:T(8,128)} custom-call(f32[4]{0:T(128)} %density.3, f32[8,32,512]{2,1,0:T(8,128)} %background_in.3, s32[8,32,512]{2,1,0:T(8,128)} %sites_in.3, f32[1,256]{1,0:T(1,128)} %log_param_in.3, f32[4,1,256]{2,1,0:T(1,128)} %dirs_in.3), custom_call_target="tpu_custom_call" | custom-call | tf_op jit(solution)/shard_map/packet/pallas_call | solution.py:753
  5.9 1.3 %collective-permute-start.1 = (f32[100,8,128]{2,1,0:T(8,128)}, f32[100,8,128]{2,1,0:T(8,128)S(1)}, u32[]{:S(2)}, u32[]{:S(2)}) collective-permute-start(f32[100,8,128]{2,1,0:T(8,128)} %packet.1), channel_id=1, source_target_pairs={{1,0},{2,1},{3,2},{4,3},{5,4},{6,5},{7,6},{8,7},{9,8},{10,9},{11,1... | collective-permute-start | bytes 1228808 | tf_op jit(solution)/shard_map/ppermute | solution.py:763
  7.2 0.0 copy-start.2
  7.3 0.0 copy-start.3
  7.3 0.0 copy-start.4
  7.3 0.1 add_convert_fusion.edge
  7.4 0.0 collective-permute-done.beyond
  7.4 0.0 copy-done
  7.4 0.0 copy-done.1
  7.4 0.6 %copy-done.2 = f32[4,1,256]{2,1,0:T(1,128)S(1)} copy-done((f32[4,1,256]{2,1,0:T(1,128)S(1)}, f32[4,1,256]{2,1,0:T(1,128)}, u32[]{:S(2)}) %copy-start.2) | copy-done | bytes 4120
  7.9 0.0 copy-done.3
  7.9 0.0 copy-done.4
  7.9 6.0 %inner.1 = (f32[128,8,128]{2,1,0:T(8,128)S(1)}, f32[144,8,128]{2,1,0:T(8,128)S(1)}, f32[4,8,128]{2,1,0:T(8,128)S(1)}, f32[4,4,16,8,128]{4,3,2,1,0:T(8,128)S(1)},...) custom-call(s32[2]{0:T(128)S(1)} %add_convert_fusion.edge, f32[4]{0:T(128)S(1)} %copy-done.4, ...), custom_call_target="tpu_custom_call" | custom-call | flops 1000000000 | bytes 16777216 | tf_op jit(solution)/shard_map/inner/pallas_call | solution.py:765
  14.0 0.0 collective-permute-done.1.packet
  14.0 4.7 %outer.1 = f32[16,2,8,128]{3,2,1,0:T(8,128)S(1)} custom-call(s32[2]{0:T(128)S(1)} %add_convert_fusion.edge, f32[128,8,128]{2,1,0:T(8,128)S(1)} %get-tuple-element.8.own_coef, f32[144,8,128]{2,1,0:T(8,128)S(1)} %get-tuple-element.9.own_src, f32[4,8,128]{2,1,0:T(8,128)S(1)} %get-tuple-element.10.own_wide, f32[4,4,16,8,128]{4,3,2,1,0:T(8,128)S(1)} %get-tuple-element.11.kept, ...), custom_call_target="tpu_custom_call" | custom-call | tf_op jit(solution)/shard_map/outer/pallas_call | solution.py:787
  18.7 17.2 %all_to_all.5 = f32[16,2,8,128]{3,2,1,0:T(8,128)S(1)} all-to-all(f32[16,2,8,128]{3,2,1,0:T(8,128)S(1)} %outer.1), channel_id=1, replica_groups={{0,2,4,6,8,10,12,14,16,18,20,22,24,26,28,30},{1,3,5,7,9,11,13,15,17,19,..., dimensions={0} | all-to-all | bytes 262144 | tf_op jit(solution)/shard_map/all_to_all | solution.py:805
  35.9 0.3 collective-permute-start.2
  36.2 0.1 pad_add_fusion.place
  36.2 1.0 %collective-permute-done.2 = f32[16,2,8,128]{3,2,1,0:T(8,128)S(1)} collective-permute-done((f32[16,2,8,128]{3,2,1,0:T(8,128)S(1)}, f32[16,2,8,128]{3,2,1,0:T(8,128)S(1)}, u32[]{:S(2)}, u32[]{:S(2)}) %collective-permute-start.2) | collective-permute-done | bytes 131104 | tf_op jit(solution)/shard_map/ppermute | solution.py:808
  37.2 1.6 %factor.1 = (f32[4,1,256]{2,1,0:T(1,128)}, f32[8,8]{1,0:T(8,128)}) custom-call(s32[2]{0:T(128)S(1)} %pad_add_fusion.place, f32[256,128]{1,0:T(8,128)S(1)} %bitcast.6, f32[256,128]{1,0:T(8,128)S(1)} %bitcast.7), custom_call_target="tpu_custom_call" | custom-call | tf_op jit(solution)/shard_map/factor/pallas_call | solution.py:818
Async XLA Ops:
  1.6 5.7 %copy-start = (f32[8,32,512]{2,1,0:T(8,128)S(1)}, f32[8,32,512]{2,1,0:T(8,128)}, u32[]{:S(2)}) copy-start(f32[8,32,512]{2,1,0:T(8,128)} %background_in.3) | copy-start | bytes 1572868
  1.6 5.7 %copy-start.1 = (s32[8,32,512]{2,1,0:T(8,128)S(1)}, s32[8,32,512]{2,1,0:T(8,128)}, u32[]{:S(2)}) copy-start(s32[8,32,512]{2,1,0:T(8,128)} %sites_in.3) | copy-start | bytes 1572868
  1.7 5.7 %collective-permute-start = (f32[5,32,512]{2,1,0:T(8,128)S(1)}, f32[5,32,512]{2,1,0:T(8,128)S(1)}, u32[]{:S(2)}, u32[]{:S(2)}) collective-permute-start(f32[5,32,512]{2,1,0:T(8,128)S(1)} %slice.3), channel_id=1, source_target_pairs={{1,0},{2,1},{3,2},{4,3},{5,4},{6,5},{7,6},{8,7},{9,8},{10,9},{11,1... | collective-permute-start | bytes 983048 | tf_op jit(solution)/shard_map/ppermute | solution.py:751
  5.9 8.0 %collective-permute-start.1 = (f32[100,8,128]{2,1,0:T(8,128)}, f32[100,8,128]{2,1,0:T(8,128)S(1)}, u32[]{:S(2)}, u32[]{:S(2)}) collective-permute-start(f32[100,8,128]{2,1,0:T(8,128)} %packet.1), channel_id=1, source_target_pairs={{1,0},{2,1},{3,2},{4,3},{5,4},{6,5},{7,6},{8,7},{9,8},{10,9},{11,1... | collective-permute-start | bytes 1228808 | tf_op jit(solution)/shard_map/ppermute | solution.py:763
  7.2 0.7 %copy-start.2 = (f32[4,1,256]{2,1,0:T(1,128)S(1)}, f32[4,1,256]{2,1,0:T(1,128)}, u32[]{:S(2)}) copy-start(f32[4,1,256]{2,1,0:T(1,128)} %dirs_in.3) | copy-start | bytes 12292
  7.3 0.7 %copy-start.3 = (f32[1,256]{1,0:T(1,128)S(1)}, f32[1,256]{1,0:T(1,128)}, u32[]{:S(2)}) copy-start(f32[1,256]{1,0:T(1,128)} %log_param_in.3) | copy-start | bytes 3076
  7.3 0.7 %copy-start.4 = (f32[4]{0:T(128)S(1)}, f32[4]{0:T(128)}, u32[]{:S(2)}) copy-start(f32[4]{0:T(128)} %density.3) | copy-start | bytes 52
  35.9 1.3 %collective-permute-start.2 = (f32[16,2,8,128]{3,2,1,0:T(8,128)S(1)}, f32[16,2,8,128]{3,2,1,0:T(8,128)S(1)}, u32[]{:S(2)}, u32[]{:S(2)}) collective-permute-start(f32[16,2,8,128]{3,2,1,0:T(8,128)S(1)} %all_to_all.5), channel_id=1, source_target_pairs={{0,1},{1,0},{2,3},{3,2},{4,5},{5,4},{6,7},{7,6},{8,9},{9,8},{10,11... | collective-permute-start | bytes 393224 | tf_op jit(solution)/shard_map/ppermute | solution.py:808

commit v5 on v2

--- a/solution.py
+++ b/solution.py
@@ -12,6 +12,7 @@
 REF = 8
 STEP = 0.12
 HALO = 3
+RAW_SITES = 3
 LANES = 128
 HIGHEST = lax.Precision.HIGHEST
 
@@ -133,7 +134,7 @@
 
 def packet_kernel(
     density, background_in, sites_in, log_param_in, dirs_in, packet,
-    background, sites, log_param, dirs, order, bg, site, made, sems, out_sems,
+    background, sites, log_param, dirs, order, bg, site, made, sems,
 ):
     count, rows, columns = sites.shape
     chunks, folds = columns // LANES, rows // 8
@@ -142,8 +143,8 @@
     pairs = [
         (log_param_in, log_param),
         (dirs_in, dirs),
-        (background_in.at[pl.ds(count - 1, 1)], background),
-        (sites_in.at[pl.ds(0, count)], sites),
+        (background_in.at[pl.ds(2 * HALO - 1, 1)], background),
+        (sites_in.at[pl.ds(2 * HALO - count, count)], sites),
     ]
     copies = [pltpu.make_async_copy(a, b, sems.at[n]) for n, (a, b) in enumerate(pairs)]
     for copy in copies:
@@ -152,23 +153,14 @@
     copies[0].wait()
     copies[1].wait()
     spread = spread_cells(dirs, log_param, folds, chunks)
-    for p in range(probes):
+    for p in range(probes + 1):
         made[p] = spread[p]
     copies[2].wait()
     copies[3].wait()
     placed = interleave([flat(background[...])], [flat(sites[...]).astype(jnp.float32)], order)
     keep(placed[0], bg)
     keep(placed[1], site)
-    sent = []
-
-    def send(start, stop):
-        at = pl.ds(start, stop - start)
-        copy = pltpu.make_async_copy(made.at[at], packet.at[at], out_sems.at[len(sent)])
-        copy.start()
-        sent.append(copy)
-
-    first = probes + tiles
-    middle = first + (count - 1) // 2 * tiles
+    first = probes + 1 + tiles
     for z in range(count):
         for r in range(folds):
             for k in range(chunks):
@@ -177,14 +169,11 @@
                 if z < count - 1:
                     made[first + z * tiles + t] = trap
                 else:
-                    made[probes + t] = source_of(trap, bg[k, tile_rows(0, r, rows, folds), :])
-        if z == (count - 1) // 2 - 1:
-            send(first, middle)
-        elif z == count - 2:
-            send(middle, first + (count - 1) * tiles)
-    send(0, first)
-    for copy in sent:
-        copy.wait()
+                    source = source_of(trap, bg[k, tile_rows(0, r, rows, folds), :])
+                    made[probes + 1 + t] = source
+    sent = pltpu.make_async_copy(made, packet, sems.at[4])
+    sent.start()
+    sent.wait()
 
 
 class Steps:
@@ -384,9 +373,9 @@
 
 
 def inner_kernel(
-    edge, density, background_in, sites_in, log_param_in, dirs_in, beyond,
-    coef, src, wide, kept, sums, next_bg,
-    background, sites, log_param, dirs, order, bg, far, site, even, odd, sems,
+    edge, density, background_in, sites_in, log_param_in, dirs_in,
+    coef, src, wide, kept, sums, order,
+    background, sites, log_param, dirs, bg, site, even, odd, sems,
 ):
     planes, rows, columns = background.shape
     chunks, folds = columns // LANES, rows // 8
@@ -413,10 +402,8 @@
     for p in range(probes):
         wide[p] = spread[p]
 
-    placed = interleave(
-        [flat(background[...]), flat(beyond[...])], [flat(sites[...]).astype(jnp.float32)], order
-    )
-    for x, scratch in zip(placed, (bg, far, site)):
+    placed = interleave([flat(background[...])], [flat(sites[...]).astype(jnp.float32)], order)
+    for x, scratch in zip(placed, (bg, site)):
         keep(x, scratch)
     for r in range(folds):
         for k in range(chunks):
@@ -426,8 +413,6 @@
                 trap = trap_of(density, site[k, at, :]) * spread[probes]
                 coef[z * tiles + t] = weight_of(trap)
                 src[z * tiles + t] = source_of(trap, bg[k, at, :])
-            for z in range(beyond.shape[0]):
-                next_bg[z * tiles + t] = far[k, tile_rows(z, r, rows, folds), :]
     at_low = edge[0] != 0
 
     def low(z):
@@ -448,8 +433,21 @@
         sums[p] = result[p]
 
 
+def beyond_kernel(rows, folds, order, raw, next_bg, next_site, bg, site):
+    chunks = bg.shape[0]
+    tiles = chunks * folds
+    count = bg.shape[1]
+    placed = interleave([raw[:count, :]], [raw[count:, :]], order)
+    for x, scratch, to in zip(placed, (bg, site), (next_bg, next_site)):
+        keep(x, scratch)
+        for z in range(to.shape[0] // tiles):
+            for t in range(tiles):
+                r, k = t // chunks, t % chunks
+                to[z * tiles + t] = scratch[k, tile_rows(z, r, rows, folds), :]
+
+
 def outer_kernel(
-    chunks, folds, edge, own_coef, own_src, own_wide, kept, own_sums, next_bg, packet, out,
+    chunks, folds, edge, density, own_coef, own_src, own_wide, kept, own_sums, next_bg, next_site, packet, out,
     coef, src, even, odd,
 ):
     tiles = chunks * folds
@@ -472,16 +470,28 @@
     copy(own_src, own, src, own, planes - last + HALO)
     copy(own_coef, own, coef, own, planes - last + HALO)
 
+    raw = next_site.shape[0]
+    scale = packet[probes]
+
     def beyond_plane(n, carry):
         for t in range(tiles):
             at = n * tiles + t
-            trap = packet[probes + tiles + at]
+            trap = trap_of(density, next_site[at]) * scale
             coef[halo + at] = weight_of(trap)
             src[halo + at] = source_of(trap, next_bg[at])
         return carry
 
-    lax.fori_loop(0, 2 * HALO - 1, beyond_plane, 0)
-    copy(packet, probes, src, (total - 1) * tiles, 1)
+    def packet_plane(n, carry):
+        for t in range(tiles):
+            at = n * tiles + t
+            trap = packet[probes + 1 + tiles + at - raw]
+            coef[halo + at] = weight_of(trap)
+            src[halo + at] = source_of(trap, next_bg[at])
+        return carry
+
+    lax.fori_loop(0, raw // tiles, beyond_plane, 0)
+    lax.fori_loop(raw // tiles, 2 * HALO - 1, packet_plane, 0)
+    copy(packet, probes + 1, src, (total - 1) * tiles, 1)
     steps.clear(even, odd)
     for p in range(probes):
         for t in range(tiles):
@@ -729,21 +739,29 @@
         return pltpu.VMEM((chunks, held * rows, LANES), jnp.float32)
 
     down = [(i + 1, i) for i in range(slabs - 1)]
-    beyond = lax.ppermute(background[: 2 * HALO - 1], "space", down)
-    size = probes + 2 * HALO * tiles
+    near = 2 * HALO - 1
+    raw = jnp.concatenate(
+        [
+            background[:near].reshape((near * rows, columns)),
+            site_class[:RAW_SITES].reshape((RAW_SITES * rows, columns)).astype(jnp.float32),
+        ],
+        axis=0,
+    )
+    raw = lax.ppermute(raw, "space", down)
+    size = probes + 1 + (2 * HALO - RAW_SITES) * tiles
     packet = pl.pallas_call(
         packet_kernel,
         out_shape=shape(size),
         in_specs=[smem] + [anywhere] * 4,
         out_specs=anywhere,
-        scratch_shapes=inputs(1, 2 * HALO)
-        + [rows_of(1), rows_of(2 * HALO), scratch(size), copies(4), copies(3)],
+        scratch_shapes=inputs(1, 2 * HALO - RAW_SITES)
+        + [rows_of(1), rows_of(2 * HALO - RAW_SITES), scratch(size), copies(5)],
         compiler_params=params,
         name="packet",
     )(trap_density, background, site_class, log_param, probe_dirs)
     next_packet = lax.ppermute(packet, "space", down)
     edge = jnp.stack([at_space > 0, at_space < slabs - 1]).astype(jnp.int32)
-    own_coef, own_src, wide, kept, sums, next_bg = pl.pallas_call(
+    own_coef, own_src, wide, kept, sums, order = pl.pallas_call(
         inner_kernel,
         out_shape=(
             shape(planes * tiles),
@@ -751,24 +769,34 @@
             shape(probes),
             shape(4, probes, tiles),
             shape(probes),
-            shape((2 * HALO - 1) * tiles),
+            jax.ShapeDtypeStruct((columns, columns), jnp.bfloat16),
         ),
-        in_specs=[smem, smem] + [anywhere] * 4 + [vmem],
+        in_specs=[smem, smem] + [anywhere] * 4,
         out_specs=(vmem,) * 6,
-        scratch_shapes=inputs(planes, planes)
-        + [rows_of(planes), rows_of(2 * HALO - 1), rows_of(planes)]
+        scratch_shapes=inputs(planes, planes)[:4]
+        + [rows_of(planes), rows_of(planes)]
         + [scratch(planes + 1, probes, tiles)] * 2
         + [copies(4)],
         compiler_params=pltpu.CompilerParams(vmem_limit_bytes=28 * 2**20),
         cost_estimate=pl.CostEstimate(flops=10**9, bytes_accessed=2**24, transcendentals=256),
         name="inner",
-    )(edge, trap_density, background, site_class, log_param, probe_dirs, beyond)
+    )(edge, trap_density, background, site_class, log_param, probe_dirs)
+
+    next_bg, next_site = pl.pallas_call(
+        functools.partial(beyond_kernel, rows, folds),
+        out_shape=(shape(near * tiles), shape(RAW_SITES * tiles)),
+        in_specs=[vmem] * 2,
+        out_specs=(vmem,) * 2,
+        scratch_shapes=[rows_of(near), rows_of(RAW_SITES)],
+        compiler_params=pltpu.CompilerParams(vmem_limit_bytes=28 * 2**20),
+        name="beyond",
+    )(order, raw)
 
     pieces = probes * cells // LANES
     images = pl.pallas_call(
         functools.partial(outer_kernel, chunks, folds),
         out_shape=jax.ShapeDtypeStruct((groups * slabs // 2, 2, pieces, LANES), jnp.float32),
-        in_specs=[smem] + [vmem] * 7,
+        in_specs=[smem] * 2 + [vmem] * 8,
         out_specs=vmem,
         scratch_shapes=[
             scratch(total * tiles),
@@ -778,7 +806,7 @@
         ],
         compiler_params=pltpu.CompilerParams(vmem_limit_bytes=28 * 2**20),
         name="outer",
-    )(edge, own_coef, own_src, wide, kept, sums, next_bg, next_packet)
+    )(edge, trap_density, own_coef, own_src, wide, kept, sums, next_bg, next_site, next_packet)
 
     same = [
         [g * slabs + z for g in range(groups) for z in range(parity, slabs, 2)] for parity in (0, 1)

time: 39.1 us -> 40 us (1.023)
  other arithmetic: 0.15 us -> 1.92 us
  blocking collectives: 17.2 us -> 16.4 us
    convert_element_type x0 -> x1, other arithmetic: none -> 0.94 us  [shards(): site_class[:RAW_SITES].reshape((RAW_SITES * rows, columns))]
    concatenate x0 -> x1, other arithmetic: none -> 0.82 us  [shards(): jnp.concatenate([background[:near].reshape((near * rows, columns)), site_...]
    all_to_all x1, blocking collectives: 17.2 us -> 16.4 us  [shards(): lax.all_to_all(images, ('probe', 'space'), split_axis=0, concat_axis=0, a...]
    pallas_call x0 -> x1, Pallas kernels: none -> 0.49 us  [shards(): pl.pallas_call(functools.partial(beyond_kernel, rows, folds), out_shape=(...]
    pallas_call x1, Pallas kernels: 6.04 us -> 5.62 us  [shards(): pl.pallas_call(inner_kernel, out_shape=(shape(planes * tiles), shape((pla...]
    slice x1 -> x2, local copies, waits for them, and re-layouts: 1 us -> 0.97 us  [shards(): background[:near].reshape((near * rows, columns))]
  transfers between devices with their start and end apart: 3 -> 3, of which waited for: 1 -> 1; matrix products, arithmetic and copies ran while one was open for 0% -> 0% of each run, Pallas kernels for 23% -> 22%
where the time goes in v5:
time: 40 us; the launch traced here: 39.7 us
  blocking collectives  16.4 us (41%)
  Pallas kernels  15.1 us (38%)
  starting transfers between devices  2.71 us (7%)
  other arithmetic  1.92 us (5%)
  local copies, waits for them, and re-layouts  1.58 us (4%)
  waiting for transfers between devices  1.28 us (3%)
  between operations  0.74 us (2%)
    all_to_all x1, blocking collectives, shards(): lax.all_to_all(images, ('probe', 'space'), split_axis=0, concat_axis=0, a...  16.4 us
    pallas_call x1, Pallas kernels, shards(): pl.pallas_call(inner_kernel, out_shape=(shape(planes * tiles), shape((pla...  5.62 us
    pallas_call x1, Pallas kernels, shards(): pl.pallas_call(functools.partial(outer_kernel, chunks, folds), out_shape=...  4.78 us
    pallas_call x1, Pallas kernels, shards(): pl.pallas_call(packet_kernel, out_shape=shape(size), in_specs=[smem] + [a...  2.68 us
    pallas_call x1, Pallas kernels, shards(): pl.pallas_call(functools.partial(register_kernel, groups, slabs, probes),...  1.57 us
    ppermute x1, starting transfers between devices, shards(): raw = lax.ppermute(raw, 'space', down)  1.41 us
    ppermute x1, starting transfers between devices, shards(): next_packet = lax.ppermute(packet, 'space', down)  1.29 us
    ppermute x1, waiting for transfers between devices, shards(): other = lax.ppermute(mine, 'space', [(z, z ^ 1) for z in range(slabs)])  1.27 us
  transfers between devices with their start and end apart: 3, of which 1 were waited for; matrix products, arithmetic and copies ran while one was open for 0% of the time, Pallas kernels for 22%

profile of v5, /device:TPU:0, one launch (start us, length us, event | category | flops | bytes accessed | tf_op | source)
XLA Modules:
  0.0 39.7 jit_solution(16135124286503431840)
XLA Ops:
  0.6 0.9 %slice_convert_fusion = f32[3,32,512]{2,1,0:T(8,128)S(1)} fusion(s32[8,32,512]{2,1,0:T(8,128)} %sites_in.3), kind=kLoop, calls=%fused_computation.1 | loop fusion | flops 49152 | bytes 393216 | tf_op jit(solution)/shard_map/convert_element_type | solution.py:746
  1.6 0.0 slice-start
  1.6 1.0 %slice-done = f32[5,32,512]{2,1,0:T(8,128)S(1)} async-done(((f32[8,32,512]{2,1,0:T(8,128)}), f32[5,32,512]{2,1,0:T(8,128)S(1)}, s32[]{:S(2)}) %slice-start) | async-done | bytes 327704 | tf_op jit(solution)/shard_map/slice | solution.py:745
  2.6 0.8 %pad_maximum_fusion = f32[256,512]{1,0:T(8,128)} fusion(f32[96,512]{1,0:T(8,128)S(1)} %bitcast.11, f32[160,512]{1,0:T(8,128)S(1)} %bitcast.8), kind=kLoop, calls=%fused_computation | loop fusion | flops 131072 | bytes 1048576 | tf_op jit(solution)/shard_map/concatenate | solution.py:743
  3.4 0.0 copy-start
  3.4 0.0 copy-start.1
  3.4 1.4 %collective-permute-start = (f32[256,512]{1,0:T(8,128)}, f32[256,512]{1,0:T(8,128)S(1)}, u32[]{:S(2)}, u32[]{:S(2)}) collective-permute-start(f32[256,512]{1,0:T(8,128)} %pad_maximum_fusion), channel_id=1, source_target_pairs={{1,0},{2,1},{3,2},{4,3},{5,4},{6,5},{7,6},{8,7},{9,8},{10,9},{11,1... | collective-permute-start | bytes 1572872 | tf_op jit(solution)/shard_map/ppermute | solution.py:750
  4.8 2.7 %packet.1 = f32[53,8,128]{2,1,0:T(8,128)} custom-call(f32[4]{0:T(128)} %density.5, f32[8,32,512]{2,1,0:T(8,128)} %background_in.3, s32[8,32,512]{2,1,0:T(8,128)} %sites_in.3, f32[1,256]{1,0:T(1,128)} %log_param_in.3, f32[4,1,256]{2,1,0:T(1,128)} %dirs_in.3), custom_call_target="tpu_custom_call" | custom-call | tf_op jit(solution)/shard_map/packet/pallas_call | solution.py:752
  7.5 1.3 %collective-permute-start.1 = (f32[53,8,128]{2,1,0:T(8,128)}, f32[53,8,128]{2,1,0:T(8,128)S(1)}, u32[]{:S(2)}, u32[]{:S(2)}) collective-permute-start(f32[53,8,128]{2,1,0:T(8,128)} %packet.1), channel_id=1, source_target_pairs={{1,0},{2,1},{3,2},{4,3},{5,4},{6,5},{7,6},{8,7},{9,8},{10,9},{11,1... | collective-permute-start | bytes 651272 | tf_op jit(solution)/shard_map/ppermute | solution.py:762
  8.8 0.0 copy-start.2
  8.8 0.0 copy-start.3
  8.8 0.0 copy-start.4
  8.8 0.1 add_convert_fusion.edge
  8.9 0.0 copy-done
  8.9 0.0 copy-done.1
  8.9 0.6 %copy-done.2 = f32[4,1,256]{2,1,0:T(1,128)S(1)} copy-done((f32[4,1,256]{2,1,0:T(1,128)S(1)}, f32[4,1,256]{2,1,0:T(1,128)}, u32[]{:S(2)}) %copy-start.2) | copy-done | bytes 4120
  9.5 0.0 copy-done.3
  9.5 0.0 copy-done.4
  9.5 5.6 %inner.1 = (f32[128,8,128]{2,1,0:T(8,128)S(1)}, f32[144,8,128]{2,1,0:T(8,128)S(1)}, f32[4,8,128]{2,1,0:T(8,128)S(1)}, f32[4,4,16,8,128]{4,3,2,1,0:T(8,128)S(1)},...) custom-call(s32[2]{0:T(128)S(1)} %add_convert_fusion.edge, f32[4]{0:T(128)S(1)} %copy-done.3, ...), custom_call_target="tpu_custom_call" | custom-call | flops 1000000000 | bytes 16777216 | tf_op jit(solution)/shard_map/inner/pallas_call | solution.py:764
  15.1 0.0 collective-permute-done.raw
  15.1 0.5 %beyond.1 = (f32[80,8,128]{2,1,0:T(8,128)S(1)}, f32[48,8,128]{2,1,0:T(8,128)S(1)}) custom-call(bf16[512,512]{1,0:T(8,128)(2,1)S(1)} %get-tuple-element.15.order, f32[256,512]{1,0:T(8,128)S(1)} %collective-permute-done.raw), custom_call_target="tpu_custom_call" | custom-call | tf_op jit(solution)/shard_map/beyond/pallas_call | solution.py:785
  15.6 0.0 collective-permute-done.1.packet
  15.7 4.8 %outer.1 = f32[16,2,8,128]{3,2,1,0:T(8,128)S(1)} custom-call(s32[2]{0:T(128)S(1)} %add_convert_fusion.edge, f32[4]{0:T(128)S(1)} %copy-done.3, f32[128,8,128]{2,1,0:T(8,128)S(1)} %get-tuple-element.10.own_coef, f32[144,8,128]{2,1,0:T(8,128)S(1)} %get-tuple-element.11.own_src, f32[4,8,128]{2,1,0:T(8,128)S(1)} %get-tuple-element.12.own_wide, ...), custom_call_target="tpu_custom_call" | custom-call | tf_op jit(solution)/shard_map/outer/pallas_call | solution.py:796
  20.4 16.4 %all_to_all.5 = f32[16,2,8,128]{3,2,1,0:T(8,128)S(1)} all-to-all(f32[16,2,8,128]{3,2,1,0:T(8,128)S(1)} %outer.1), channel_id=1, replica_groups={{0,2,4,6,8,10,12,14,16,18,20,22,24,26,28,30},{1,3,5,7,9,11,13,15,17,19,..., dimensions={0} | all-to-all | bytes 262144 | tf_op jit(solution)/shard_map/all_to_all | solution.py:814
  36.8 0.0 collective-permute-start.2
  36.8 0.1 pad_add_fusion.place
  36.9 1.3 %collective-permute-done.2 = f32[16,2,8,128]{3,2,1,0:T(8,128)S(1)} collective-permute-done((f32[16,2,8,128]{3,2,1,0:T(8,128)S(1)}, f32[16,2,8,128]{3,2,1,0:T(8,128)S(1)}, u32[]{:S(2)}, u32[]{:S(2)}) %collective-permute-start.2) | collective-permute-done | bytes 131104 | tf_op jit(solution)/shard_map/ppermute | solution.py:817
  38.1 1.6 %factor.1 = (f32[4,1,256]{2,1,0:T(1,128)}, f32[8,8]{1,0:T(8,128)}) custom-call(s32[2]{0:T(128)S(1)} %pad_add_fusion.place, f32[256,128]{1,0:T(8,128)S(1)} %bitcast.9, f32[256,128]{1,0:T(8,128)S(1)} %bitcast.10), custom_call_target="tpu_custom_call" | custom-call | tf_op jit(solution)/shard_map/factor/pallas_call | solution.py:827
Async XLA Ops:
  1.6 1.0 %slice-start = ((f32[8,32,512]{2,1,0:T(8,128)}), f32[5,32,512]{2,1,0:T(8,128)S(1)}, s32[]{:S(2)}) async-start(f32[8,32,512]{2,1,0:T(8,128)} %background_in.3), calls=%async_computation.1 | async-start | bytes 655360 | tf_op jit(solution)/shard_map/slice | solution.py:745
  3.4 5.5 %copy-start = (f32[8,32,512]{2,1,0:T(8,128)S(1)}, f32[8,32,512]{2,1,0:T(8,128)}, u32[]{:S(2)}) copy-start(f32[8,32,512]{2,1,0:T(8,128)} %background_in.3) | copy-start | bytes 1572868
  3.4 5.5 %copy-start.1 = (s32[8,32,512]{2,1,0:T(8,128)S(1)}, s32[8,32,512]{2,1,0:T(8,128)}, u32[]{:S(2)}) copy-start(s32[8,32,512]{2,1,0:T(8,128)} %sites_in.3) | copy-start | bytes 1572868
  3.4 11.8 %collective-permute-start = (f32[256,512]{1,0:T(8,128)}, f32[256,512]{1,0:T(8,128)S(1)}, u32[]{:S(2)}, u32[]{:S(2)}) collective-permute-start(f32[256,512]{1,0:T(8,128)} %pad_maximum_fusion), channel_id=1, source_target_pairs={{1,0},{2,1},{3,2},{4,3},{5,4},{6,5},{7,6},{8,7},{9,8},{10,9},{11,1... | collective-permute-start | bytes 1572872 | tf_op jit(solution)/shard_map/ppermute | solution.py:750
  7.5 8.2 %collective-permute-start.1 = (f32[53,8,128]{2,1,0:T(8,128)}, f32[53,8,128]{2,1,0:T(8,128)S(1)}, u32[]{:S(2)}, u32[]{:S(2)}) collective-permute-start(f32[53,8,128]{2,1,0:T(8,128)} %packet.1), channel_id=1, source_target_pairs={{1,0},{2,1},{3,2},{4,3},{5,4},{6,5},{7,6},{8,7},{9,8},{10,9},{11,1... | collective-permute-start | bytes 651272 | tf_op jit(solution)/shard_map/ppermute | solution.py:762
  8.8 0.7 %copy-start.2 = (f32[4,1,256]{2,1,0:T(1,128)S(1)}, f32[4,1,256]{2,1,0:T(1,128)}, u32[]{:S(2)}) copy-start(f32[4,1,256]{2,1,0:T(1,128)} %dirs_in.3) | copy-start | bytes 12292
  8.8 0.7 %copy-start.3 = (f32[4]{0:T(128)S(1)}, f32[4]{0:T(128)}, u32[]{:S(2)}) copy-start(f32[4]{0:T(128)} %density.5) | copy-start | bytes 52
  8.8 0.7 %copy-start.4 = (f32[1,256]{1,0:T(1,128)S(1)}, f32[1,256]{1,0:T(1,128)}, u32[]{:S(2)}) copy-start(f32[1,256]{1,0:T(1,128)} %log_param_in.3) | copy-start | bytes 3076
  36.8 1.3 %collective-permute-start.2 = (f32[16,2,8,128]{3,2,1,0:T(8,128)S(1)}, f32[16,2,8,128]{3,2,1,0:T(8,128)S(1)}, u32[]{:S(2)}, u32[]{:S(2)}) collective-permute-start(f32[16,2,8,128]{3,2,1,0:T(8,128)S(1)} %all_to_all.5), channel_id=1, source_target_pairs={{0,1},{1,0},{2,3},{3,2},{4,5},{5,4},{6,7},{7,6},{8,9},{9,8},{10,11... | collective-permute-start | bytes 393224 | tf_op jit(solution)/shard_map/ppermute | solution.py:817

commit v6 on v2

--- a/solution.py
+++ b/solution.py
@@ -263,29 +263,39 @@
         down, here, there, up = at(z - 1), at(z), at(z + 1), at(z + 2)
         for p in range(self.probes):
             pair = [[ref[plane, p, t] for t in range(tiles)] for plane in (here, there)]
-            for r in range(folds):
-                for k in range(chunks):
-                    t = r * chunks + k
-                    for n, value in enumerate(pair):
-                        left = value[t - 1] if k else self.from_left(value[t + chunks - 1])
-                        if k + 1 < chunks:
-                            right = value[t + 1]
-                        else:
-                            right = self.from_right(value[t + 1 - chunks])
-                        if r:
-                            before = value[t - chunks]
-                        else:
-                            before = self.from_before(value[t + tiles - chunks])
-                        if r + 1 < folds:
-                            after = value[t + chunks]
-                        else:
-                            after = self.from_after(value[t + chunks - tiles])
+            for n, value in enumerate(pair):
+                shared = self.corners(value)
+                for r in range(folds):
+                    for k in range(chunks):
+                        t = r * chunks + k
                         above = pair[1 - n][t] + (ref[up, p, t] if n else ref[down, p, t])
                         weight = self.coef[(z + n) * tiles + t]
                         if extra:
                             weight = weight + extra
-                        sides = (left + right) + (before + after)
+                        sides = shared[r, k] + shared[r + 1, k + 1]
                         emit(z + n, p, t, (sides + above) + weight * value[t])
+
+    def corners(self, value):
+        chunks, folds = self.chunks, self.folds
+
+        def at(r, k):
+            if r < 0:
+                return self.from_before(value[(folds - 1) * chunks + k])
+            if r == folds:
+                return self.from_after(value[k])
+            if k < 0:
+                return self.from_left(value[r * chunks + chunks - 1])
+            if k == chunks:
+                return self.from_right(value[r * chunks])
+            return value[r * chunks + k]
+
+        ends = ((folds, 0), (0, chunks))
+        return {
+            (r, k): at(r - 1, k) + at(r, k - 1)
+            for r in range(folds + 1)
+            for k in range(chunks + 1)
+            if (r, k) not in ends
+        }
 
     def step(self, ref, to, valid, wanted, extra=0.0):
         start, stop = wanted

time: 39.1 us -> 39 us (level)
  no operation moved by 1% of the time
where the time goes in v6:
time: 39 us; the launch traced here: 38.7 us
  blocking collectives  17.3 us (44%)
  Pallas kernels  14.9 us (38%)
  starting transfers between devices  2.97 us (8%)
  local copies, waits for them, and re-layouts  1.59 us (4%)
  waiting for transfers between devices  1.02 us (3%)
  between operations  0.74 us (2%)
    all_to_all x1, blocking collectives, shards(): lax.all_to_all(images, ('probe', 'space'), split_axis=0, concat_axis=0, a...  17.3 us
    pallas_call x1, Pallas kernels, shards(): pl.pallas_call(inner_kernel, out_shape=(shape(planes * tiles), shape((pla...  5.9 us
    pallas_call x1, Pallas kernels, shards(): pl.pallas_call(functools.partial(outer_kernel, chunks, folds), out_shape=...  4.58 us
    pallas_call x1, Pallas kernels, shards(): pl.pallas_call(packet_kernel, out_shape=shape(size), in_specs=[smem] + [a...  2.84 us
    pallas_call x1, Pallas kernels, shards(): pl.pallas_call(functools.partial(register_kernel, groups, slabs, probes),...  1.57 us
    ppermute x1, starting transfers between devices, shards(): beyond = lax.ppermute(background[:2 * HALO - 1], 'space', down)  1.42 us
    ppermute x1, starting transfers between devices, shards(): next_packet = lax.ppermute(packet, 'space', down)  1.29 us
    ppermute x1, waiting for transfers between devices, shards(): other = lax.ppermute(mine, 'space', [(z, z ^ 1) for z in range(slabs)])  1.01 us
  transfers between devices with their start and end apart: 3, of which 1 were waited for; matrix products, arithmetic and copies ran while one was open for 0% of the time, Pallas kernels for 23%

profile of v6, /device:TPU:0, one launch (start us, length us, event | category | flops | bytes accessed | tf_op | source)
XLA Modules:
  0.0 38.7 jit_solution(3453278990047925365)
XLA Ops:
  0.6 1.0 %slice.3 = f32[5,32,512]{2,1,0:T(8,128)S(1)} slice(f32[8,32,512]{2,1,0:T(8,128)} %background_in.3), slice={[0:5], [0:32], [0:512]} | slice | bytes 655360 | tf_op jit(solution)/shard_map/slice | solution.py:742
  1.6 0.0 copy-start
  1.6 0.0 copy-start.1
  1.7 1.4 %collective-permute-start = (f32[5,32,512]{2,1,0:T(8,128)S(1)}, f32[5,32,512]{2,1,0:T(8,128)S(1)}, u32[]{:S(2)}, u32[]{:S(2)}) collective-permute-start(f32[5,32,512]{2,1,0:T(8,128)S(1)} %slice.3), channel_id=1, source_target_pairs={{1,0},{2,1},{3,2},{4,3},{5,4},{6,5},{7,6},{8,7},{9,8},{10,9},{11,1... | collective-permute-start | bytes 983048 | tf_op jit(solution)/shard_map/ppermute | solution.py:742
  3.1 2.8 %packet.1 = f32[100,8,128]{2,1,0:T(8,128)} custom-call(f32[4]{0:T(128)} %density.3, f32[8,32,512]{2,1,0:T(8,128)} %background_in.3, s32[8,32,512]{2,1,0:T(8,128)} %sites_in.3, f32[1,256]{1,0:T(1,128)} %log_param_in.3, f32[4,1,256]{2,1,0:T(1,128)} %dirs_in.3), custom_call_target="tpu_custom_call" | custom-call | tf_op jit(solution)/shard_map/packet/pallas_call | solution.py:744
  5.9 1.3 %collective-permute-start.1 = (f32[100,8,128]{2,1,0:T(8,128)}, f32[100,8,128]{2,1,0:T(8,128)S(1)}, u32[]{:S(2)}, u32[]{:S(2)}) collective-permute-start(f32[100,8,128]{2,1,0:T(8,128)} %packet.1), channel_id=1, source_target_pairs={{1,0},{2,1},{3,2},{4,3},{5,4},{6,5},{7,6},{8,7},{9,8},{10,9},{11,1... | collective-permute-start | bytes 1228808 | tf_op jit(solution)/shard_map/ppermute | solution.py:754
  7.2 0.0 copy-start.2
  7.3 0.0 copy-start.3
  7.3 0.0 copy-start.4
  7.3 0.1 add_convert_fusion.edge
  7.4 0.0 collective-permute-done.beyond
  7.4 0.0 copy-done
  7.4 0.0 copy-done.1
  7.4 0.6 %copy-done.2 = f32[4,1,256]{2,1,0:T(1,128)S(1)} copy-done((f32[4,1,256]{2,1,0:T(1,128)S(1)}, f32[4,1,256]{2,1,0:T(1,128)}, u32[]{:S(2)}) %copy-start.2) | copy-done | bytes 4120
  7.9 0.0 copy-done.3
  7.9 0.0 copy-done.4
  7.9 5.9 %inner.1 = (f32[128,8,128]{2,1,0:T(8,128)S(1)}, f32[144,8,128]{2,1,0:T(8,128)S(1)}, f32[4,8,128]{2,1,0:T(8,128)S(1)}, f32[4,4,16,8,128]{4,3,2,1,0:T(8,128)S(1)},...) custom-call(s32[2]{0:T(128)S(1)} %add_convert_fusion.edge, f32[4]{0:T(128)S(1)} %copy-done.4, ...), custom_call_target="tpu_custom_call" | custom-call | flops 1000000000 | bytes 16777216 | tf_op jit(solution)/shard_map/inner/pallas_call | solution.py:756
  13.9 0.0 collective-permute-done.1.packet
  13.9 4.6 %outer.1 = f32[16,2,8,128]{3,2,1,0:T(8,128)S(1)} custom-call(s32[2]{0:T(128)S(1)} %add_convert_fusion.edge, f32[128,8,128]{2,1,0:T(8,128)S(1)} %get-tuple-element.8.own_coef, f32[144,8,128]{2,1,0:T(8,128)S(1)} %get-tuple-element.9.own_src, f32[4,8,128]{2,1,0:T(8,128)S(1)} %get-tuple-element.10.own_wide, f32[4,4,16,8,128]{4,3,2,1,0:T(8,128)S(1)} %get-tuple-element.11.kept, ...), custom_call_target="tpu_custom_call" | custom-call | tf_op jit(solution)/shard_map/outer/pallas_call | solution.py:778
  18.5 17.3 %all_to_all.5 = f32[16,2,8,128]{3,2,1,0:T(8,128)S(1)} all-to-all(f32[16,2,8,128]{3,2,1,0:T(8,128)S(1)} %outer.1), channel_id=1, replica_groups={{0,2,4,6,8,10,12,14,16,18,20,22,24,26,28,30},{1,3,5,7,9,11,13,15,17,19,..., dimensions={0} | all-to-all | bytes 262144 | tf_op jit(solution)/shard_map/all_to_all | solution.py:796
  35.8 0.3 collective-permute-start.2
  36.0 0.1 pad_add_fusion.place
  36.1 1.0 %collective-permute-done.2 = f32[16,2,8,128]{3,2,1,0:T(8,128)S(1)} collective-permute-done((f32[16,2,8,128]{3,2,1,0:T(8,128)S(1)}, f32[16,2,8,128]{3,2,1,0:T(8,128)S(1)}, u32[]{:S(2)}, u32[]{:S(2)}) %collective-permute-start.2) | collective-permute-done | bytes 131104 | tf_op jit(solution)/shard_map/ppermute | solution.py:799
  37.1 1.6 %factor.1 = (f32[4,1,256]{2,1,0:T(1,128)}, f32[8,8]{1,0:T(8,128)}) custom-call(s32[2]{0:T(128)S(1)} %pad_add_fusion.place, f32[256,128]{1,0:T(8,128)S(1)} %bitcast.6, f32[256,128]{1,0:T(8,128)S(1)} %bitcast.7), custom_call_target="tpu_custom_call" | custom-call | tf_op jit(solution)/shard_map/factor/pallas_call | solution.py:809
Async XLA Ops:
  1.6 5.7 %copy-start = (f32[8,32,512]{2,1,0:T(8,128)S(1)}, f32[8,32,512]{2,1,0:T(8,128)}, u32[]{:S(2)}) copy-start(f32[8,32,512]{2,1,0:T(8,128)} %background_in.3) | copy-start | bytes 1572868
  1.6 5.7 %copy-start.1 = (s32[8,32,512]{2,1,0:T(8,128)S(1)}, s32[8,32,512]{2,1,0:T(8,128)}, u32[]{:S(2)}) copy-start(s32[8,32,512]{2,1,0:T(8,128)} %sites_in.3) | copy-start | bytes 1572868
  1.7 5.7 %collective-permute-start = (f32[5,32,512]{2,1,0:T(8,128)S(1)}, f32[5,32,512]{2,1,0:T(8,128)S(1)}, u32[]{:S(2)}, u32[]{:S(2)}) collective-permute-start(f32[5,32,512]{2,1,0:T(8,128)S(1)} %slice.3), channel_id=1, source_target_pairs={{1,0},{2,1},{3,2},{4,3},{5,4},{6,5},{7,6},{8,7},{9,8},{10,9},{11,1... | collective-permute-start | bytes 983048 | tf_op jit(solution)/shard_map/ppermute | solution.py:742
  5.9 7.9 %collective-permute-start.1 = (f32[100,8,128]{2,1,0:T(8,128)}, f32[100,8,128]{2,1,0:T(8,128)S(1)}, u32[]{:S(2)}, u32[]{:S(2)}) collective-permute-start(f32[100,8,128]{2,1,0:T(8,128)} %packet.1), channel_id=1, source_target_pairs={{1,0},{2,1},{3,2},{4,3},{5,4},{6,5},{7,6},{8,7},{9,8},{10,9},{11,1... | collective-permute-start | bytes 1228808 | tf_op jit(solution)/shard_map/ppermute | solution.py:754
  7.2 0.7 %copy-start.2 = (f32[4,1,256]{2,1,0:T(1,128)S(1)}, f32[4,1,256]{2,1,0:T(1,128)}, u32[]{:S(2)}) copy-start(f32[4,1,256]{2,1,0:T(1,128)} %dirs_in.3) | copy-start | bytes 12292
  7.3 0.7 %copy-start.3 = (f32[1,256]{1,0:T(1,128)S(1)}, f32[1,256]{1,0:T(1,128)}, u32[]{:S(2)}) copy-start(f32[1,256]{1,0:T(1,128)} %log_param_in.3) | copy-start | bytes 3076
  7.3 0.7 %copy-start.4 = (f32[4]{0:T(128)S(1)}, f32[4]{0:T(128)}, u32[]{:S(2)}) copy-start(f32[4]{0:T(128)} %density.3) | copy-start | bytes 52
  35.8 1.3 %collective-permute-start.2 = (f32[16,2,8,128]{3,2,1,0:T(8,128)S(1)}, f32[16,2,8,128]{3,2,1,0:T(8,128)S(1)}, u32[]{:S(2)}, u32[]{:S(2)}) collective-permute-start(f32[16,2,8,128]{3,2,1,0:T(8,128)S(1)} %all_to_all.5), channel_id=1, source_target_pairs={{0,1},{1,0},{2,3},{3,2},{4,5},{5,4},{6,7},{7,6},{8,9},{9,8},{10,11... | collective-permute-start | bytes 393224 | tf_op jit(solution)/shard_map/ppermute | solution.py:799

commit v7 on v6

--- a/solution.py
+++ b/solution.py
@@ -261,6 +261,11 @@
             return jnp.where((z >= first) & (z < stop), z, self.zero_plane)
 
         down, here, there, up = at(z - 1), at(z), at(z + 1), at(z + 2)
+        raised = {}
+        if extra:
+            for n in (0, 1):
+                for t in range(tiles):
+                    raised[n, t] = self.coef[(z + n) * tiles + t] + extra
         for p in range(self.probes):
             pair = [[ref[plane, p, t] for t in range(tiles)] for plane in (here, there)]
             for n, value in enumerate(pair):
@@ -269,9 +274,7 @@
                     for k in range(chunks):
                         t = r * chunks + k
                         above = pair[1 - n][t] + (ref[up, p, t] if n else ref[down, p, t])
-                        weight = self.coef[(z + n) * tiles + t]
-                        if extra:
-                            weight = weight + extra
+                        weight = raised[n, t] if extra else self.coef[(z + n) * tiles + t]
                         sides = shared[r, k] + shared[r + 1, k + 1]
                         emit(z + n, p, t, (sides + above) + weight * value[t])
 

time: 39 us -> 39 us (level)
  no operation moved by 1% of the time
where the time goes in v7:
time: 39 us; the launch traced here: 38.7 us
  blocking collectives  17.3 us (44%)
  Pallas kernels  14.9 us (38%)
  starting transfers between devices  2.97 us (8%)
  local copies, waits for them, and re-layouts  1.59 us (4%)
  waiting for transfers between devices  1.02 us (3%)
  between operations  0.74 us (2%)
    all_to_all x1, blocking collectives, shards(): lax.all_to_all(images, ('probe', 'space'), split_axis=0, concat_axis=0, a...  17.3 us
    pallas_call x1, Pallas kernels, shards(): pl.pallas_call(inner_kernel, out_shape=(shape(planes * tiles), shape((pla...  5.91 us
    pallas_call x1, Pallas kernels, shards(): pl.pallas_call(functools.partial(outer_kernel, chunks, folds), out_shape=...  4.57 us
    pallas_call x1, Pallas kernels, shards(): pl.pallas_call(packet_kernel, out_shape=shape(size), in_specs=[smem] + [a...  2.84 us
    pallas_call x1, Pallas kernels, shards(): pl.pallas_call(functools.partial(register_kernel, groups, slabs, probes),...  1.57 us
    ppermute x1, starting transfers between devices, shards(): beyond = lax.ppermute(background[:2 * HALO - 1], 'space', down)  1.42 us
    ppermute x1, starting transfers between devices, shards(): next_packet = lax.ppermute(packet, 'space', down)  1.29 us
    ppermute x1, waiting for transfers between devices, shards(): other = lax.ppermute(mine, 'space', [(z, z ^ 1) for z in range(slabs)])  1.01 us
  transfers between devices with their start and end apart: 3, of which 1 were waited for; matrix products, arithmetic and copies ran while one was open for 0% of the time, Pallas kernels for 23%

profile of v7, /device:TPU:0, one launch (start us, length us, event | category | flops | bytes accessed | tf_op | source)
XLA Modules:
  0.0 38.7 jit_solution(14205943752116108724)
XLA Ops:
  0.6 1.0 %slice.3 = f32[5,32,512]{2,1,0:T(8,128)S(1)} slice(f32[8,32,512]{2,1,0:T(8,128)} %background_in.3), slice={[0:5], [0:32], [0:512]} | slice | bytes 655360 | tf_op jit(solution)/shard_map/slice | solution.py:745
  1.6 0.0 copy-start
  1.6 0.0 copy-start.1
  1.7 1.4 %collective-permute-start = (f32[5,32,512]{2,1,0:T(8,128)S(1)}, f32[5,32,512]{2,1,0:T(8,128)S(1)}, u32[]{:S(2)}, u32[]{:S(2)}) collective-permute-start(f32[5,32,512]{2,1,0:T(8,128)S(1)} %slice.3), channel_id=1, source_target_pairs={{1,0},{2,1},{3,2},{4,3},{5,4},{6,5},{7,6},{8,7},{9,8},{10,9},{11,1... | collective-permute-start | bytes 983048 | tf_op jit(solution)/shard_map/ppermute | solution.py:745
  3.1 2.8 %packet.1 = f32[100,8,128]{2,1,0:T(8,128)} custom-call(f32[4]{0:T(128)} %density.3, f32[8,32,512]{2,1,0:T(8,128)} %background_in.3, s32[8,32,512]{2,1,0:T(8,128)} %sites_in.3, f32[1,256]{1,0:T(1,128)} %log_param_in.3, f32[4,1,256]{2,1,0:T(1,128)} %dirs_in.3), custom_call_target="tpu_custom_call" | custom-call | tf_op jit(solution)/shard_map/packet/pallas_call | solution.py:747
  5.9 1.3 %collective-permute-start.1 = (f32[100,8,128]{2,1,0:T(8,128)}, f32[100,8,128]{2,1,0:T(8,128)S(1)}, u32[]{:S(2)}, u32[]{:S(2)}) collective-permute-start(f32[100,8,128]{2,1,0:T(8,128)} %packet.1), channel_id=1, source_target_pairs={{1,0},{2,1},{3,2},{4,3},{5,4},{6,5},{7,6},{8,7},{9,8},{10,9},{11,1... | collective-permute-start | bytes 1228808 | tf_op jit(solution)/shard_map/ppermute | solution.py:757
  7.2 0.0 copy-start.2
  7.3 0.0 copy-start.3
  7.3 0.0 copy-start.4
  7.3 0.1 add_convert_fusion.edge
  7.4 0.0 collective-permute-done.beyond
  7.4 0.0 copy-done
  7.4 0.0 copy-done.1
  7.4 0.6 %copy-done.2 = f32[4,1,256]{2,1,0:T(1,128)S(1)} copy-done((f32[4,1,256]{2,1,0:T(1,128)S(1)}, f32[4,1,256]{2,1,0:T(1,128)}, u32[]{:S(2)}) %copy-start.2) | copy-done | bytes 4120
  7.9 0.0 copy-done.3
  7.9 0.0 copy-done.4
  7.9 5.9 %inner.1 = (f32[128,8,128]{2,1,0:T(8,128)S(1)}, f32[144,8,128]{2,1,0:T(8,128)S(1)}, f32[4,8,128]{2,1,0:T(8,128)S(1)}, f32[4,4,16,8,128]{4,3,2,1,0:T(8,128)S(1)},...) custom-call(s32[2]{0:T(128)S(1)} %add_convert_fusion.edge, f32[4]{0:T(128)S(1)} %copy-done.4, ...), custom_call_target="tpu_custom_call" | custom-call | flops 1000000000 | bytes 16777216 | tf_op jit(solution)/shard_map/inner/pallas_call | solution.py:759
  13.9 0.0 collective-permute-done.1.packet
  13.9 4.6 %outer.1 = f32[16,2,8,128]{3,2,1,0:T(8,128)S(1)} custom-call(s32[2]{0:T(128)S(1)} %add_convert_fusion.edge, f32[128,8,128]{2,1,0:T(8,128)S(1)} %get-tuple-element.8.own_coef, f32[144,8,128]{2,1,0:T(8,128)S(1)} %get-tuple-element.9.own_src, f32[4,8,128]{2,1,0:T(8,128)S(1)} %get-tuple-element.10.own_wide, f32[4,4,16,8,128]{4,3,2,1,0:T(8,128)S(1)} %get-tuple-element.11.kept, ...), custom_call_target="tpu_custom_call" | custom-call | tf_op jit(solution)/shard_map/outer/pallas_call | solution.py:781
  18.5 17.3 %all_to_all.5 = f32[16,2,8,128]{3,2,1,0:T(8,128)S(1)} all-to-all(f32[16,2,8,128]{3,2,1,0:T(8,128)S(1)} %outer.1), channel_id=1, replica_groups={{0,2,4,6,8,10,12,14,16,18,20,22,24,26,28,30},{1,3,5,7,9,11,13,15,17,19,..., dimensions={0} | all-to-all | bytes 262144 | tf_op jit(solution)/shard_map/all_to_all | solution.py:799
  35.7 0.3 collective-permute-start.2
  36.0 0.1 pad_add_fusion.place
  36.1 1.0 %collective-permute-done.2 = f32[16,2,8,128]{3,2,1,0:T(8,128)S(1)} collective-permute-done((f32[16,2,8,128]{3,2,1,0:T(8,128)S(1)}, f32[16,2,8,128]{3,2,1,0:T(8,128)S(1)}, u32[]{:S(2)}, u32[]{:S(2)}) %collective-permute-start.2) | collective-permute-done | bytes 131104 | tf_op jit(solution)/shard_map/ppermute | solution.py:802
  37.1 1.6 %factor.1 = (f32[4,1,256]{2,1,0:T(1,128)}, f32[8,8]{1,0:T(8,128)}) custom-call(s32[2]{0:T(128)S(1)} %pad_add_fusion.place, f32[256,128]{1,0:T(8,128)S(1)} %bitcast.6, f32[256,128]{1,0:T(8,128)S(1)} %bitcast.7), custom_call_target="tpu_custom_call" | custom-call | tf_op jit(solution)/shard_map/factor/pallas_call | solution.py:812
Async XLA Ops:
  1.6 5.7 %copy-start = (f32[8,32,512]{2,1,0:T(8,128)S(1)}, f32[8,32,512]{2,1,0:T(8,128)}, u32[]{:S(2)}) copy-start(f32[8,32,512]{2,1,0:T(8,128)} %background_in.3) | copy-start | bytes 1572868
  1.6 5.7 %copy-start.1 = (s32[8,32,512]{2,1,0:T(8,128)S(1)}, s32[8,32,512]{2,1,0:T(8,128)}, u32[]{:S(2)}) copy-start(s32[8,32,512]{2,1,0:T(8,128)} %sites_in.3) | copy-start | bytes 1572868
  1.7 5.7 %collective-permute-start = (f32[5,32,512]{2,1,0:T(8,128)S(1)}, f32[5,32,512]{2,1,0:T(8,128)S(1)}, u32[]{:S(2)}, u32[]{:S(2)}) collective-permute-start(f32[5,32,512]{2,1,0:T(8,128)S(1)} %slice.3), channel_id=1, source_target_pairs={{1,0},{2,1},{3,2},{4,3},{5,4},{6,5},{7,6},{8,7},{9,8},{10,9},{11,1... | collective-permute-start | bytes 983048 | tf_op jit(solution)/shard_map/ppermute | solution.py:745
  5.9 7.9 %collective-permute-start.1 = (f32[100,8,128]{2,1,0:T(8,128)}, f32[100,8,128]{2,1,0:T(8,128)S(1)}, u32[]{:S(2)}, u32[]{:S(2)}) collective-permute-start(f32[100,8,128]{2,1,0:T(8,128)} %packet.1), channel_id=1, source_target_pairs={{1,0},{2,1},{3,2},{4,3},{5,4},{6,5},{7,6},{8,7},{9,8},{10,9},{11,1... | collective-permute-start | bytes 1228808 | tf_op jit(solution)/shard_map/ppermute | solution.py:757
  7.2 0.7 %copy-start.2 = (f32[4,1,256]{2,1,0:T(1,128)S(1)}, f32[4,1,256]{2,1,0:T(1,128)}, u32[]{:S(2)}) copy-start(f32[4,1,256]{2,1,0:T(1,128)} %dirs_in.3) | copy-start | bytes 12292
  7.3 0.7 %copy-start.3 = (f32[1,256]{1,0:T(1,128)S(1)}, f32[1,256]{1,0:T(1,128)}, u32[]{:S(2)}) copy-start(f32[1,256]{1,0:T(1,128)} %log_param_in.3) | copy-start | bytes 3076
  7.3 0.7 %copy-start.4 = (f32[4]{0:T(128)S(1)}, f32[4]{0:T(128)}, u32[]{:S(2)}) copy-start(f32[4]{0:T(128)} %density.3) | copy-start | bytes 52
  35.7 1.3 %collective-permute-start.2 = (f32[16,2,8,128]{3,2,1,0:T(8,128)S(1)}, f32[16,2,8,128]{3,2,1,0:T(8,128)S(1)}, u32[]{:S(2)}, u32[]{:S(2)}) collective-permute-start(f32[16,2,8,128]{3,2,1,0:T(8,128)S(1)} %all_to_all.5), channel_id=1, source_target_pairs={{0,1},{1,0},{2,3},{3,2},{4,5},{5,4},{6,7},{7,6},{8,9},{9,8},{10,11... | collective-permute-start | bytes 393224 | tf_op jit(solution)/shard_map/ppermute | solution.py:802
